TPU v7x, 32 devices: a whole 2x2x4 slice. The times are simulated.
32 devices in a mesh: dp: 16 (over z, x, core), seq: 2 (over y).
Axes of the slice: x: 2, y: 2, z: 4, core: 2. Of those that a mesh axis runs over, the one named last changes fastest.
Arguments:
- block_in: bfloat16 [16, 256, 1024], P('dp', 'seq'), may hold values from -6 to 6
- conditioning: bfloat16 [16, 768], P('dp'), may hold values from -6 to 6
- crop_ids: int32 [16, 256], P('dp', 'seq'), may hold values from 0 to 15, as said below
- positions: int32 [16, 2, 256], P('dp', None, 'seq'), may hold values from 0 to 15
- qkv_weight: bfloat16 [1024, 3072], P(('dp', 'seq')), may hold values from -0.1875 to 0.1875
- out_weight: bfloat16 [1024, 1024], P(('dp', 'seq')), may hold values from -0.75 to 0.75
- up_weight: bfloat16 [1024, 6144], P(('dp', 'seq')), may hold values from -0.1875 to 0.1875
- down_weight: bfloat16 [3072, 1024], P(('dp', 'seq')), may hold values from -0.109375 to 0.109375
- attn_modulate: bfloat16 [768, 1024], P(('dp', 'seq')), may hold values from -0.0546875 to 0.0546875
- ffn_modulate: bfloat16 [768, 1024], P(('dp', 'seq')), may hold values from -0.0546875 to 0.0546875
- head_scale: float32 [16], replicated, may hold values from 6 to 20
- cotangent: bfloat16 [16, 256, 1024], P('dp', 'seq'), may hold values from -6 to 6
Outputs:
- block_out: bfloat16 [16, 256, 1024], P('dp', 'seq')
- input_grad: float32 [16, 256, 1024], P('dp', 'seq')
- cond_grad: float32 [16, 768], P('dp')
- qkv_grad: float32 [1024, 3072], P(('dp', 'seq'))
- out_grad: float32 [1024, 1024], P(('dp', 'seq'))
- up_grad: float32 [1024, 6144], P(('dp', 'seq'))
- down_grad: float32 [3072, 1024], P(('dp', 'seq'))
- attnmod_grad: float32 [768, 1024], P(('dp', 'seq'))
- ffnmod_grad: float32 [768, 1024], P(('dp', 'seq'))
- scale_grad: float32 [16], replicated
Inputs may be any that keep to these rules, and one draw needn't show every extreme that they name: `crop_ids`: in every canvas each crop id from 0 to 15 labels exactly 16 tokens, and the first and the last token of a canvas carry the same crop id.
All inputs are finite; a program needn't handle non-finite values.
Results may differ from a plain program's by a relative error of at most 0.03.
Values may be sent and summed in bfloat16 or wider, within the bound.
A program may use at most 256 MiB of HBM per device.

v0:
```python
import math

import jax
import jax.numpy as jnp
from jax import lax
from jax.sharding import PartitionSpec as P

eps_norm = 1e-06
eps_cosine = 1e-06
negative = -1e30
key_rows = 256


def block_split(count, limit):
    size_rows = math.gcd(count, limit)
    return (size_rows, count // size_rows)


def rope_tables(positions, heads):
    unit_pos = (2.0 * positions.astype(jnp.float32) + 1.0) / 16.0 - 1.0
    exponent = (
        jnp.arange(8, dtype=jnp.float32)[None, :] * heads
        + jnp.arange(heads, dtype=jnp.float32)[:, None]
    ) / (8.0 * heads)
    frequency = math.pi * 10.0**exponent
    angles = jnp.moveaxis(unit_pos[..., None, None] * frequency, -4, -2)
    return (jnp.cos(angles), jnp.sin(angles))


def rotate(vector, cosine, sine):
    leading = vector.shape[:-1]
    turned_part = vector[..., :32].reshape(leading + (2, 2, 8))
    first_half = turned_part[..., 0, :]
    second_half = turned_part[..., 1, :]
    turned = jnp.stack(
        [first_half * cosine - second_half * sine, first_half * sine + second_half * cosine],
        axis=-2,
    )
    return jnp.concatenate([turned.reshape(leading + (32,)), vector[..., 32:]], axis=-1)


def norm_forward(value, scale):
    inverse = lax.rsqrt(jnp.mean(value * value, axis=-1, keepdims=True) + eps_norm)
    return (value * inverse * scale[:, None], inverse)


def norm_backward(value, inverse, scale, grad_norm):
    scaled = grad_norm * scale[:, None]
    grad_value = inverse * scaled - value * inverse**3 * jnp.mean(
        scaled * value, axis=-1, keepdims=True
    )
    grad_scale = jnp.sum(grad_norm * value * inverse, axis=1)
    return (grad_value, grad_scale)


def cosine_forward(value, root_scale):
    factor = root_scale[:, None] * lax.rsqrt(
        jnp.sum(value * value, axis=-1, keepdims=True) + eps_cosine
    )
    return (value * factor, factor)


def cosine_backward(value, factor, grad):
    squares = jnp.sum(value * value, axis=-1, keepdims=True) + eps_cosine
    along = jnp.sum(grad * value, axis=-1, keepdims=True)
    grad_value = factor * grad - value * factor * along / squares
    return (grad_value, jnp.sum(along * factor, axis=(0, 1, 3)))


def geglu(value_part, gate_part):
    return value_part * jax.nn.gelu(gate_part, approximate=False)


def pair_grads(queries, grad_att, log_total, deltas, query_crop, key_block, value_block, key_crop):
    scores = jnp.einsum("cqhd,ckhd->cqhk", queries, key_block, preferred_element_type=jnp.float32)
    allowed = (query_crop[:, :, None] == key_crop[:, None, :])[:, :, None, :]
    probs = jnp.exp(jnp.where(allowed, scores - log_total[..., None], negative))
    probs = jnp.where(allowed, probs, 0.0)
    dotted = jnp.einsum(
        "cqhd,ckhd->cqhk", grad_att, value_block, preferred_element_type=jnp.float32
    )
    slope = (probs * (dotted - deltas[..., None])).astype(jnp.bfloat16)
    grad_q = jnp.einsum("cqhk,ckhd->cqhd", slope, key_block, preferred_element_type=jnp.float32)
    grad_k = jnp.einsum("cqhk,cqhd->ckhd", slope, queries, preferred_element_type=jnp.float32)
    grad_v = jnp.einsum(
        "cqhk,cqhd->ckhd", probs.astype(jnp.bfloat16), grad_att, preferred_element_type=jnp.float32
    )
    return (grad_q, grad_k, grad_v)


def pack_terms(terms, lead_shape):
    return jnp.concatenate([term.reshape(lead_shape + (-1,)) for term in terms], axis=-1)


def unpack_terms(packed_row, terms, owners):
    results = []
    offset = 0
    for term in terms:
        own_rows = term.shape[0] // owners
        count = own_rows * term.shape[1]
        results.append(packed_row[offset : offset + count].reshape(own_rows, term.shape[1]))
        offset = offset + count
    return results


def shards(
    block_in,
    conditioning,
    crop_ids,
    positions,
    qkv_weight,
    out_weight,
    up_weight,
    down_weight,
    attn_modulate,
    ffn_modulate,
    head_scale,
    cotangent,
):
    qkv_full, out_full, up_full, down_full, attn_mod, ffn_mod = (
        lax.all_gather(qkv_weight, ("dp", "seq"), axis=0, tiled=True),
        lax.all_gather(out_weight, ("dp", "seq"), axis=0, tiled=True),
        lax.all_gather(up_weight, ("dp", "seq"), axis=0, tiled=True),
        lax.all_gather(down_weight, ("dp", "seq"), axis=0, tiled=True),
        lax.all_gather(attn_modulate, ("dp", "seq"), axis=0, tiled=True),
        lax.all_gather(ffn_modulate, ("dp", "seq"), axis=0, tiled=True),
    )
    canvases, rows, width = block_in.shape
    heads = head_scale.shape[0]
    head_size = width // heads
    hidden_width = down_full.shape[0]
    seq_count = lax.axis_size("seq")
    inputs = block_in.astype(jnp.float32)
    scale_attn = 1.0 + jnp.dot(conditioning, attn_mod, preferred_element_type=jnp.float32)
    scale_ffn = 1.0 + jnp.dot(conditioning, ffn_mod, preferred_element_type=jnp.float32)
    normed_attn, inverse_attn = norm_forward(inputs, scale_attn)
    normed_attn = normed_attn.astype(jnp.bfloat16)
    qkv_all = jnp.einsum(
        "csd,de->cse", normed_attn, qkv_full, preferred_element_type=jnp.float32
    ).reshape(canvases, rows, 3, heads, head_size)
    root_scale = jnp.sqrt(head_scale)
    query_cos, query_factor = cosine_forward(qkv_all[:, :, 0], root_scale)
    key_cos, key_factor = cosine_forward(qkv_all[:, :, 1], root_scale)
    cosine, sine = rope_tables(positions, heads)
    queries = rotate(query_cos, cosine, sine).astype(jnp.bfloat16)
    keys_flat = rotate(key_cos, cosine, sine).astype(jnp.bfloat16).reshape(canvases, rows, width)
    values_flat = qkv_all[:, :, 2].astype(jnp.bfloat16).reshape(canvases, rows, width)
    start_state = (
        jnp.full((canvases, rows, heads), negative, jnp.float32),
        jnp.zeros((canvases, rows, heads), jnp.float32),
        jnp.zeros((canvases, rows, heads, head_size), jnp.float32),
    )
    state_now = start_state
    piece_keys = lax.all_gather(keys_flat, "seq", axis=1, tiled=True)
    piece_values = lax.all_gather(values_flat, "seq", axis=1, tiled=True)
    piece_crop = lax.all_gather(crop_ids, "seq", axis=1, tiled=True)
    size_rows, number = block_split(piece_keys.shape[1], key_rows)

    def step_block(state, block_index):
        running_max, row_total, weighted = state
        offset = block_index * size_rows
        key_block = lax.dynamic_slice_in_dim(piece_keys, offset, size_rows, 1).reshape(
            canvases, size_rows, heads, head_size
        )
        value_block = lax.dynamic_slice_in_dim(piece_values, offset, size_rows, 1).reshape(
            canvases, size_rows, heads, head_size
        )
        crop_block = lax.dynamic_slice_in_dim(piece_crop, offset, size_rows, 1)
        scores = jnp.einsum(
            "cqhd,ckhd->cqhk", queries, key_block, preferred_element_type=jnp.float32
        )
        allowed = (crop_ids[:, :, None] == crop_block[:, None, :])[:, :, None, :]
        scores = jnp.where(allowed, scores, negative)
        new_max = jnp.maximum(running_max, jnp.max(scores, axis=-1))
        weights = jnp.where(allowed, jnp.exp(scores - new_max[..., None]), 0.0)
        shrink = jnp.exp(running_max - new_max)
        row_total = row_total * shrink + jnp.sum(weights, axis=-1)
        weighted = weighted * shrink[..., None] + jnp.einsum(
            "cqhk,ckhd->cqhd",
            weights.astype(jnp.bfloat16),
            value_block,
            preferred_element_type=jnp.float32,
        )
        return ((new_max, row_total, weighted), None)

    state_now, unused = lax.scan(step_block, state_now, jnp.arange(number))
    running_max, row_total, weighted = state_now
    log_total = running_max + jnp.log(row_total)
    attended_raw = weighted / row_total[..., None]
    attended = attended_raw.astype(jnp.bfloat16).reshape(canvases, rows, width)
    middle = inputs + jnp.einsum(
        "csd,de->cse", attended, out_full, preferred_element_type=jnp.float32
    )
    normed_ffn, inverse_ffn = norm_forward(middle, scale_ffn)
    normed_ffn = normed_ffn.astype(jnp.bfloat16)
    up_all = jnp.einsum("csd,de->cse", normed_ffn, up_full, preferred_element_type=jnp.float32)
    value_part = up_all[..., :hidden_width]
    gate_part = up_all[..., hidden_width:]
    hidden = geglu(value_part, gate_part).astype(jnp.bfloat16)
    block_out = (
        middle + jnp.einsum("csf,fd->csd", hidden, down_full, preferred_element_type=jnp.float32)
    ).astype(jnp.bfloat16)
    down_term = jnp.einsum("csf,csd->fd", hidden, cotangent, preferred_element_type=jnp.float32)
    grad_hidden = jnp.einsum(
        "csd,fd->csf", cotangent, down_full, preferred_element_type=jnp.float32
    )
    unused_value, geglu_pull = jax.vjp(geglu, value_part, gate_part)
    grad_value, grad_gate = geglu_pull(grad_hidden)
    grad_up = jnp.concatenate([grad_value, grad_gate], axis=-1).astype(jnp.bfloat16)
    up_term = jnp.einsum("csd,cse->de", normed_ffn, grad_up, preferred_element_type=jnp.float32)
    grad_normed_ffn = jnp.einsum(
        "cse,de->csd", grad_up, up_full, preferred_element_type=jnp.float32
    )
    grad_mid_norm, ffn_scale_sum = norm_backward(middle, inverse_ffn, scale_ffn, grad_normed_ffn)
    grad_middle = cotangent.astype(jnp.float32) + grad_mid_norm
    grad_branch = grad_middle.astype(jnp.bfloat16)
    out_term = jnp.einsum("csd,cse->de", attended, grad_branch, preferred_element_type=jnp.float32)
    grad_attended = (
        jnp.einsum("cse,de->csd", grad_branch, out_full, preferred_element_type=jnp.float32)
        .astype(jnp.bfloat16)
        .reshape(canvases, rows, heads, head_size)
    )
    deltas = jnp.sum(grad_attended.astype(jnp.float32) * attended_raw, axis=-1)
    start_back = (
        jnp.zeros((canvases, rows, heads, head_size), jnp.float32),
        jnp.zeros((canvases, rows * seq_count, 2 * width), jnp.float32),
    )
    state_now = start_back
    fold_piece_keys = lax.all_gather(keys_flat, "seq", axis=1, tiled=True)
    fold_piece_values = lax.all_gather(values_flat, "seq", axis=1, tiled=True)
    fold_piece_crop = lax.all_gather(crop_ids, "seq", axis=1, tiled=True)
    fold_size_rows, number = block_split(fold_piece_keys.shape[1], key_rows)

    def step_block(state, block_index):
        grad_q_sum, grad_kv_all = state
        offset = block_index * fold_size_rows
        key_block = lax.dynamic_slice_in_dim(fold_piece_keys, offset, fold_size_rows, 1).reshape(
            canvases, fold_size_rows, heads, head_size
        )
        value_block = lax.dynamic_slice_in_dim(
            fold_piece_values, offset, fold_size_rows, 1
        ).reshape(canvases, fold_size_rows, heads, head_size)
        crop_block = lax.dynamic_slice_in_dim(fold_piece_crop, offset, fold_size_rows, 1)
        grad_q, grad_k, grad_v = pair_grads(
            queries, grad_attended, log_total, deltas, crop_ids, key_block, value_block, crop_block
        )
        update = jnp.concatenate(
            [
                grad_k.reshape(canvases, fold_size_rows, width),
                grad_v.reshape(canvases, fold_size_rows, width),
            ],
            axis=-1,
        )
        previous = lax.dynamic_slice_in_dim(grad_kv_all, offset, fold_size_rows, 1)
        grad_kv_all = lax.dynamic_update_slice_in_dim(grad_kv_all, previous + update, offset, 1)
        return ((grad_q_sum + grad_q, grad_kv_all), None)

    state_now, unused = lax.scan(step_block, state_now, jnp.arange(number))
    grad_queries, grad_kv_all = state_now
    grad_kv = lax.psum_scatter(
        grad_kv_all.astype(jnp.bfloat16), "seq", scatter_dimension=1, tiled=True
    ).astype(jnp.float32)
    grad_keys = grad_kv[..., :width].reshape(canvases, rows, heads, head_size)
    grad_values = grad_kv[..., width:].reshape(canvases, rows, heads, head_size)
    grad_query_cos = rotate(grad_queries, cosine, -sine)
    grad_key_cos = rotate(grad_keys, cosine, -sine)
    grad_query_raw, query_part = cosine_backward(qkv_all[:, :, 0], query_factor, grad_query_cos)
    grad_key_raw, key_part = cosine_backward(qkv_all[:, :, 1], key_factor, grad_key_cos)
    scale_local = (query_part + key_part) / (2.0 * head_scale)
    grad_qkv = (
        jnp.stack([grad_query_raw, grad_key_raw, grad_values], axis=2)
        .astype(jnp.bfloat16)
        .reshape(canvases, rows, 3 * width)
    )
    qkv_term = jnp.einsum("csd,cse->de", normed_attn, grad_qkv, preferred_element_type=jnp.float32)
    grad_normed_attn = jnp.einsum(
        "cse,de->csd", grad_qkv, qkv_full, preferred_element_type=jnp.float32
    )
    grad_in_norm, attn_scale_sum = norm_backward(inputs, inverse_attn, scale_attn, grad_normed_attn)
    input_grad = grad_middle + grad_in_norm
    attn_sums, ffn_sums = lax.psum((attn_scale_sum, ffn_scale_sum), "seq")
    attn_sums = attn_sums.astype(jnp.bfloat16)
    ffn_sums = ffn_sums.astype(jnp.bfloat16)
    cond_grad = jnp.einsum(
        "cd,nd->cn", attn_sums, attn_mod, preferred_element_type=jnp.float32
    ) + jnp.einsum("cd,nd->cn", ffn_sums, ffn_mod, preferred_element_type=jnp.float32)
    leader = lax.axis_index("seq") == 0
    attn_mod_term = jnp.where(
        leader,
        jnp.einsum("cn,cd->nd", conditioning, attn_sums, preferred_element_type=jnp.float32),
        0.0,
    )
    ffn_mod_term = jnp.where(
        leader,
        jnp.einsum("cn,cd->nd", conditioning, ffn_sums, preferred_element_type=jnp.float32),
        0.0,
    )
    terms = (qkv_term, out_term, up_term, down_term, attn_mod_term, ffn_mod_term)
    groups = lax.axis_size("dp")
    owners = groups * seq_count
    packed = pack_terms(terms, (owners,))
    summed = lax.psum_scatter(packed, ("dp", "seq"), scatter_dimension=0, tiled=True)
    packed_row = summed[0]
    qkv_grad, out_grad, up_grad, down_grad, attnmod_grad, ffnmod_grad = unpack_terms(
        packed_row, terms, owners
    )
    scale_grad = lax.psum(scale_local, ("dp", "seq"))
    return (
        block_out,
        input_grad,
        cond_grad,
        qkv_grad,
        out_grad,
        up_grad,
        down_grad,
        attnmod_grad,
        ffnmod_grad,
        scale_grad,
    )


def solution(mesh):
    in_specs = (
        P("dp", "seq", None),
        P("dp", None),
        P("dp", "seq"),
        P("dp", None, "seq"),
        P(("dp", "seq"), None),
        P(("dp", "seq"), None),
        P(("dp", "seq"), None),
        P(("dp", "seq"), None),
        P(("dp", "seq"), None),
        P(("dp", "seq"), None),
        P(),
        P("dp", "seq", None),
    )
    out_specs = (
        P("dp", "seq", None),
        P("dp", "seq", None),
        P("dp", None),
        P(("dp", "seq"), None),
        P(("dp", "seq"), None),
        P(("dp", "seq"), None),
        P(("dp", "seq"), None),
        P(("dp", "seq"), None),
        P(("dp", "seq"), None),
        P(),
    )
    return jax.shard_map(shards, mesh=mesh, in_specs=in_specs, out_specs=out_specs, check_vma=False)
```

profile of v0, /device:TPU:0, one launch (start us, length us, event | category | flops | bytes accessed | tf_op | source)
XLA Modules:
  0.0 1495.7 jit_solution(15959884651820418867)
XLA Ops:
  8.0 0.7 all-gather.13.cloned.1.call-update
  11.9 0.7 reduce.20
  13.2 5.3 all_gather.30
  18.5 1.1 fusion.39
  20.9 0.8 broadcast_compare_fusion
  21.6 47.1 %all-gather.7.cloned.1.call-done = bf16[768,1024]{1,0:T(8,128)(2,1)} async-done(((bf16[24,1024]{1,0:T(8,128)(2,1)}), bf16[768,1024]{1,0:T(8,128)(2,1)}) %all-gather.7.cloned.1.call-update) | async-done | bytes 1572880 | tf_op jit(solution)/shard_map/all_gather | solution.py:125
  68.7 1.7 fusion.119
  70.5 55.2 %all-gather.13.cloned.1.call-done = bf16[768,1024]{1,0:T(8,128)(2,1)} async-done(((bf16[24,1024]{1,0:T(8,128)(2,1)}), bf16[768,1024]{1,0:T(8,128)(2,1)}) %all-gather.13.cloned.1.call-update) | async-done | bytes 1572880 | tf_op jit(solution)/shard_map/all_gather | solution.py:126
  125.6 1.7 fusion.117
  127.4 69.6 %all-gather.9.cloned.1.call-done = bf16[1024,3072]{1,0:T(8,128)(2,1)} async-done(((bf16[32,3072]{1,0:T(8,128)(2,1)}), bf16[1024,3072]{1,0:T(8,128)(2,1)}) %all-gather.9.cloned.1.call-update) | async-done | bytes 6291472 | tf_op jit(solution)/shard_map/all_gather | solution.py:121
  197.0 8.6 copy.65
  205.6 4.8 convolution_bitcast_fusion.2
  210.5 0.8 broadcast_add_fusion
  212.6 9.2 all_gather.33
  221.8 9.3 all_gather.34
  232.9 1.4 fusion.134
  234.4 21.0 %all-gather.11.cloned.1.call-done = bf16[1024,1024]{1,0:T(8,128)(2,1)} async-done(((bf16[32,1024]{1,0:T(8,128)(2,1)}), bf16[1024,1024]{1,0:T(8,128)(2,1)}) %all-gather.11.cloned.1.call-update) | async-done | bytes 2097168 | tf_op jit(solution)/shard_map/all_gather | solution.py:122
  255.4 2.2 multiply_reduce_fusion.1
  257.6 68.9 %all-gather.17.cloned.1.call-done = bf16[3072,1024]{1,0:T(8,128)(2,1)} async-done(((bf16[96,1024]{1,0:T(8,128)(2,1)}), bf16[3072,1024]{1,0:T(8,128)(2,1)}) %all-gather.17.cloned.1.call-update) | async-done | bytes 6291472 | tf_op jit(solution)/shard_map/all_gather | solution.py:124
  326.5 6.1 convolution_bitcast_fusion.1
  332.6 91.2 %all-gather.15.cloned.1.call-done = bf16[1024,6144]{1,0:T(8,128)(2,1)} async-done(((bf16[32,6144]{1,0:T(8,128)(2,1)}), bf16[1024,6144]{1,0:T(8,128)(2,1)}) %all-gather.15.cloned.1.call-update) | async-done | bytes 12582928 | tf_op jit(solution)/shard_map/all_gather | solution.py:123
  423.8 6.6 convolution_bitcast_fusion
  430.4 4.6 fusion.37
  435.0 2.0 fusion.38
  437.0 7.3 fusion.53
  444.3 1.5 fusion.55
  445.8 2.6 convolution_convert_fusion.2
  448.8 2.7 fusion.60
  452.6 0.9 fusion.16
  454.6 2.0 copy.91
  456.6 1.6 copy.103
  458.3 5.3 reshape.950
  463.6 10.3 fusion.34
  473.9 26.3 %reshape.951 = f32[32,196608]{1,0:T(8,128)} reshape(f32[1024,6144]{1,0:T(8,128)} %fusion.34) | data formatting | bytes 50331648 | tf_op jit(solution)/shard_map/reshape | solution.py:92
  500.2 6.3 fusion.63
  506.6 10.1 reshape.952
  517.2 1.7 reshape_bitcast_fusion
  523.1 0.9 copy-done.14
  524.0 6.5 fusion.66
  530.4 10.3 reshape.949
  540.7 10.1 constant_dynamic-update-slice_fusion.5
  550.9 4.2 fusion.47
  555.1 8.7 all-reduce.1
  563.9 3.1 select_bitcast_fusion
  567.0 2.2 reshape.953
  569.1 3.3 reshape.954
  572.5 4.4 constant_dynamic-update-slice_fusion.4
  576.9 16.8 %constant_dynamic-update-slice_fusion.3 = f32[32,475136]{1,0:T(8,128)} fusion(f32[32,475136]{1,0:T(8,128)} %constant_dynamic-update-slice_fusion.4, f32[32,196608]{1,0:T(8,128)} %reshape.951), kind=kLoop, calls=%fused_computation.193 | loop fusion | bytes 50331648
  593.7 10.0 constant_dynamic-update-slice_fusion.2
  603.7 1.9 constant_dynamic-update-slice_fusion.1
  605.6 1.1 copy-done.6
  606.7 1.9 constant_dynamic-update-slice_fusion
  609.9 5.0 fusion.21
  614.9 40.2 %psum.23 = f32[16]{0:T(128)} all-reduce(f32[16]{0:T(128)S(1)} %multiply_divide_fusion), channel_id=1, replica_groups=mesh['dp'=16,'seq'=2] {'dp','seq'}, use_global_device_ids=true, to_apply=%region_19.20 | all-reduce | flops 16 | bytes 128 | tf_op jit(solution)/shard_map/psum | solution.py:307
  655.7 2.0 convolution_reduce_fusion
  658.4 1.0 fusion.44
  659.4 805.6 %all-reduce.4.cloned.1.call-done = f32[32,475136]{1,0:T(8,128)} async-done(((f32[32,475136]{1,0:T(8,128)}), f32[32,475136]{1,0:T(8,128)}) %all-reduce.4.cloned.1.call-update) | async-done | bytes 60817424
  1465.0 5.1 dynamic-slice_reduce_fusion.1
  1470.0 0.8 reshape.955
  1470.8 1.6 dynamic-slice_reduce_fusion.3
  1473.2 10.1 dynamic-slice_reduce_fusion
  1483.3 1.0 reshape.957
  1484.3 0.8 reshape.958
  1485.1 2.0 dynamic-slice_reduce_fusion.4
  (185 shorter events, 20.7 us)
Async XLA Ops:
  7.2 118.5 %copy-start.38 = (bf16[1,768]{1,0:T(2,128)(2,1)S(1)}, bf16[1,768]{1,0:T(2,128)(2,1)}, u32[]{:S(2)}) copy-start(bf16[1,768]{1,0:T(2,128)(2,1)} %param.13) | copy-start | bytes 4612
  7.2 61.5 %all-gather.7.cloned.1.call-start = ((), (), s32[]{:S(2)}) async-start(), calls=%async_computation.1 | async-start | bytes 1622016 | tf_op jit(solution)/shard_map/all_gather | solution.py:125
  7.9 117.7 %all-gather.13.cloned.1.call-start = ((), (), s32[]{:S(2)}) async-start(), calls=%async_computation.4 | async-start | bytes 1622016 | tf_op jit(solution)/shard_map/all_gather | solution.py:126
  8.7 188.3 %all-gather.9.cloned.1.call-start = ((), (), s32[]{:S(2)}) async-start(), calls=%async_computation.2 | async-start | bytes 6488064 | tf_op jit(solution)/shard_map/all_gather | solution.py:121
  9.4 245.9 %all-gather.11.cloned.1.call-start = ((), (), s32[]{:S(2)}) async-start(), calls=%async_computation.3 | async-start | bytes 2162688 | tf_op jit(solution)/shard_map/all_gather | solution.py:122
  10.0 316.5 %all-gather.17.cloned.1.call-start = ((), (), s32[]{:S(2)}) async-start(), calls=%async_computation.6 | async-start | bytes 6488064 | tf_op jit(solution)/shard_map/all_gather | solution.py:124
  10.6 413.2 %all-gather.15.cloned.1.call-start = ((), (), s32[]{:S(2)}) async-start(), calls=%async_computation.5 | async-start | bytes 12976128 | tf_op jit(solution)/shard_map/all_gather | solution.py:123
  11.1 506.0 %reduce-scatter.4.cloned.1.call-start = ((), (), s32[]{:S(2)}) async-start(), calls=%async_computation.7 | async-start | bytes 1572864
  20.1 185.5 %copy-start.43 = (f32[128]{0:T(128)}, f32[128]{0:T(128)S(1)}, u32[]{:S(2)}) copy-start(f32[128]{0:T(128)S(1)} %get-tuple-element.120) | copy-start | bytes 1540
  20.8 191.1 %copy-start.45 = (f32[2,128]{1,0:T(2,128)}, f32[2,128]{1,0:T(2,128)S(1)}, u32[]{:S(2)}) copy-start(f32[2,128]{1,0:T(2,128)S(1)} %add_bitcast_fusion) | copy-start | bytes 3076
  20.8 191.1 %copy-start.34 = (f32[16,8]{1,0:T(8,128)}, f32[16,8]{1,0:T(8,128)S(1)}, u32[]{:S(2)}) copy-start(f32[16,8]{1,0:T(8,128)S(1)} %power_multiply_fusion) | copy-start | bytes 1540
  197.0 8.6 copy-start.7
  210.4 1.2 copy-start
  211.3 0.6 copy-start.32
  221.8 9.8 copy-start.18
  231.1 1.3 copy-start.29
  231.1 0.8 copy-start.25
  231.6 1.3 copy-start.8
  234.4 23.2 %copy-start.27 = (bf16[1,128,16,64]{1,3,2,0:T(8,128)(2,1)}, bf16[1,128,16,64]{1,3,2,0:T(8,128)(2,1)S(1)}, u32[]{:S(2)}) copy-start(bf16[1,128,16,64]{1,3,2,0:T(8,128)(2,1)S(1)} %get-tuple-element.125) | copy-start | bytes 786436
  255.4 71.1 %copy-start.22 = (bf16[1,128,1024]{2,1,0:T(8,128)(2,1)S(1)}, bf16[1,128,1024]{2,1,0:T(8,128)(2,1)}, u32[]{:S(2)}) copy-start(bf16[1,128,1024]{2,1,0:T(8,128)(2,1)} %param.23) | copy-start | bytes 786436
  257.5 166.2 %copy-start.2 = (f32[1,128,1024]{2,1,0:T(8,128)}, f32[1,128,1024]{2,1,0:T(8,128)S(1)}, u32[]{:S(2)}) copy-start(f32[1,128,1024]{2,1,0:T(8,128)S(1)} %get-tuple-element.128) | copy-start | bytes 1572868
  257.6 186.7 %copy-start.39 = (f32[128]{0:T(128)}, f32[128]{0:T(128)S(1)}, u32[]{:S(2)}) copy-start(f32[128]{0:T(128)S(1)} %get-tuple-element.122) | copy-start | bytes 1540
  423.8 6.6 copy-start.5
  423.8 13.2 slice-start
  423.8 13.2 slice-start.1
  430.4 6.6 slice-start.2
  445.8 3.0 copy-start.10
  445.8 3.0 copy-start.28
  448.7 2.7 copy-start.9
  451.4 1.0 copy-start.31
  451.4 1.2 copy-start.30
  452.6 0.9 copy-start.26
  453.5 1.0 copy-start.20
  458.2 5.4 copy-start.3
  458.2 5.3 copy-start.15
  458.2 5.3 copy-start.16
  458.2 5.3 copy-start.40
  458.2 1006.7 %all-reduce.4.cloned.1.call-start = ((), (), s32[]{:S(2)}) async-start(), calls=%async_computation.8 | async-start | bytes 121634816
  473.9 26.3 %copy-start.12 = (bf16[128,3072]{1,0:T(8,128)(2,1)S(1)}, bf16[128,3072]{1,0:T(8,128)(2,1)}, u32[]{:S(2)}) copy-start(bf16[128,3072]{1,0:T(8,128)(2,1)} %get-tuple-element.87) | copy-start | bytes 2359300
  473.9 26.3 %copy-start.23 = (bf16[1,128,1024]{2,1,0:T(8,128)(2,1)S(1)}, bf16[1,128,1024]{2,1,0:T(8,128)(2,1)}, u32[]{:S(2)}) copy-start(bf16[1,128,1024]{2,1,0:T(8,128)(2,1)} %param.23) | copy-start | bytes 786436
  506.6 10.1 copy-start.19
  506.6 10.1 copy-start.21
  519.9 1.0 copy-start.35
  519.9 1.0 copy-start.46
  520.9 1.4 copy-start.1
  521.6 1.0 copy-start.33
  521.6 1.0 copy-start.36
  521.6 1.0 copy-start.37
  522.6 1.4 copy-start.44
  523.1 0.9 copy-start.14
  530.4 20.4 %slice-start.3 = ((s8[6291456]{0:T(1024)(128)(4,1)}), s8[2097152]{0:T(1024)(128)(4,1)S(1)}, s32[]{:S(2)}) async-start(s8[6291456]{0:T(1024)(128)(4,1)} %bitcast.440), calls=%async_computation.12 | async-start | bytes 4194304
  540.7 10.1 slice-start.4
  550.8 4.2 copy-start.41
  550.8 13.1 copy-start.42
  603.7 3.0 copy-start.6
  608.6 0.7 copy-start.47
  608.6 1.1 copy-start.4
  608.6 1.3 copy-start.13
  609.9 45.3 %copy-start.17 = (bf16[768,1024]{1,0:T(8,128)(2,1)S(1)}, bf16[768,1024]{1,0:T(8,128)(2,1)}, u32[]{:S(2)}) copy-start(bf16[768,1024]{1,0:T(8,128)(2,1)} %all-gather.7.cloned.1.call-done) | copy-start | bytes 4718596
  655.2 3.2 copy-start.11
  655.2 3.2 copy-start.24
  655.2 3.2 copy-start.48
Sparse Core Ops, SparseCore 0:
  10.9 57.7 all-gather.6
  71.6 53.9 all-gather.12
  128.5 68.3 all-gather.8
  199.9 55.3 all-gather.10
  258.1 68.3 all-gather.16
  329.2 94.4 all-gather.14
  458.3 18.5 reduce-scatter.3
  608.8 856.1 all-reduce.3
where the time goes:
time: 1500 us
  waiting for transfers between devices  1160 us (77%)
  local copies, waits for them, and re-layouts  150 us (10%)
  matrix products  74.8 us (5%)
  blocking collectives  72.7 us (5%)
  other arithmetic  20.4 us (1%)
  between operations  15.4 us (1%)
    unnamed x10, waiting for transfers between devices  809 us
    all_gather x1, waiting for transfers between devices, shards(): lax.all_gather(up_weight, ('dp', 'seq'), axis=0, tiled=True)  91.2 us
    all_gather x1, waiting for transfers between devices, shards(): lax.all_gather(qkv_weight, ('dp', 'seq'), axis=0, tiled=True)  69.6 us
    all_gather x1, waiting for transfers between devices, shards(): lax.all_gather(down_weight, ('dp', 'seq'), axis=0, tiled=True)  68.9 us
    reshape x6, local copies, waits for them, and re-layouts, pack_terms(): term.reshape(lead_shape + (-1,))  57.5 us
    unnamed x118, local copies, waits for them, and re-layouts  55.5 us
    all_gather x1, waiting for transfers between devices, shards(): lax.all_gather(ffn_modulate, ('dp', 'seq'), axis=0, tiled=True)  55.2 us
    all_gather x1, waiting for transfers between devices, shards(): lax.all_gather(attn_modulate, ('dp', 'seq'), axis=0, tiled=True)  47.1 us
  transfers between devices with their start and end apart: 8, of which 7 were waited for; matrix products, arithmetic and copies ran while one was open for 7% of the time, Pallas kernels for 0%

commit v1 on v0

--- a/solution.py
+++ b/solution.py
@@ -1,8 +1,14 @@
+import functools
 import math
+import types
 
 import jax
 import jax.numpy as jnp
+import ml_dtypes
+import numpy as np
 from jax import lax
+from jax.experimental import pallas as pl
+from jax.experimental.pallas import tpu as pltpu
 from jax.sharding import PartitionSpec as P
 
 eps_norm = 1e-06
@@ -319,6 +325,1049 @@
     )
 
 
+MESH = pl.DeviceIdType.MESH
+BF = jnp.bfloat16
+F32 = jnp.float32
+PLANE = ((1, 0, 0), (0, 0, 1), (1, 0, 1), (0, 1, 0), (1, 1, 0), (0, 1, 1), (1, 1, 1))
+CHIPS = ((1, 0), (0, 1), (1, 1))
+ERF_P = (
+    0.00022905065861350646,
+    0.0034082910107109506,
+    0.050955695062380861,
+    0.18520832239976145,
+    1.128379143519084,
+)
+ERF_Q = (
+    -1.1791602954361697e-7,
+    0.000023547966471313185,
+    0.0010179625278914885,
+    0.014070470171167667,
+    0.11098505178285362,
+    0.49746925110067538,
+    1.0,
+)
+
+
+def erf(value):
+    value = jnp.clip(value, -3.832506856900711, 3.832506856900711)
+    square = value * value
+    top = jnp.full_like(value, ERF_P[0])
+    for term in ERF_P[1:]:
+        top = top * square + term
+    bottom = jnp.full_like(value, ERF_Q[0])
+    for term in ERF_Q[1:]:
+        bottom = bottom * square + term
+    return value * top / bottom
+
+
+def dot(lhs, rhs, on_lhs=1, on_rhs=0):
+    return lax.dot_general(
+        lhs, rhs, (((on_lhs,), (on_rhs,)), ((), ())), preferred_element_type=F32
+    )
+
+
+def block_kernel(
+    lines,
+    x_ref,
+    cot_ref,
+    qkv_ref,
+    up_ref,
+    out_ref,
+    down_ref,
+    amod_ref,
+    fmod_ref,
+    cond_ref,
+    crop_ref,
+    pos_ref,
+    scale_ref,
+    table_ref,
+    block_out,
+    input_grad,
+    cond_grad,
+    qkv_grad,
+    out_grad,
+    up_grad,
+    down_grad,
+    amod_grad,
+    fmod_grad,
+    scale_grad,
+    *scratch,
+):
+    names = list(scratch_plan(lines, x_ref, qkv_ref, up_ref, out_ref, down_ref))
+    s = types.SimpleNamespace(**dict(zip(names, scratch)))
+    dp = lax.axis_index("dp")
+    y = lax.axis_index("seq")
+    z = dp // 4
+    x = (dp // 2) % 2
+    c = dp % 2
+    rows, width = x_ref.shape
+    own_cols = qkv_ref.shape[2]
+    lanes = own_cols // 3
+    half_head = out_ref.shape[0]
+    hidden = up_ref.shape[2] // 2
+    down_rows = down_ref.shape[0]
+    up_rows = up_ref.shape[1]
+    mod_rows = amod_ref.shape[0]
+    canvas_rows = 2 * rows
+    crops = canvas_rows // 16
+    me = 4 * x + 2 * c + y
+    device_index = 8 * z + me
+
+    def member(step):
+        return 4 * ((x + step[0]) % 2) + 2 * ((c + step[1]) % 2) + (y + step[2]) % 2
+
+    def device(step, along=0):
+        return (
+            ((z + along) % lines) * 4 + ((x + step[0]) % 2) * 2 + (c + step[1]) % 2,
+            (y + step[2]) % 2,
+        )
+
+    here = (0, 0, 0)
+    core = (0, 1, 0)
+    sends = []
+
+    class Copy:
+        def __init__(self, src, dst_there, dst_here, sems, at, target):
+            self.out = pltpu.make_async_remote_copy(
+                src_ref=src,
+                dst_ref=dst_there,
+                send_sem=sems.at[0, at],
+                recv_sem=sems.at[1, at],
+                device_id=target,
+                device_id_type=MESH,
+            )
+            self.into = pltpu.make_async_remote_copy(
+                src_ref=src,
+                dst_ref=dst_here,
+                send_sem=sems.at[0, at],
+                recv_sem=sems.at[1, at],
+                device_id=target,
+                device_id_type=MESH,
+            )
+
+        def start(self):
+            self.out.start()
+            sends.append(self.out)
+
+        def arrive(self):
+            self.into.wait_recv()
+
+    class Gather:
+        def __init__(self, buffer, sems):
+            self.buffer = buffer
+            at = lambda step: buffer.at[member(step)]
+            self.across = [
+                Copy(at(here), at(here), at((dx, 0, dy)), sems, k, device((dx, 0, dy)))
+                for k, (dx, dy) in enumerate(CHIPS)
+            ]
+            self.pair = Copy(at(here), at(here), at(core), sems, 3, device(core))
+            self.forward = [
+                Copy(at((dx, 0, dy)), at((dx, 0, dy)), at((dx, 1, dy)), sems, 4 + k, device(core))
+                for k, (dx, dy) in enumerate(CHIPS)
+            ]
+
+        def start(self):
+            for copy in self.across:
+                copy.start()
+            self.pair.start()
+
+        def middle(self):
+            for copy, onward in zip(self.across, self.forward):
+                copy.arrive()
+                onward.start()
+
+        def finish(self):
+            self.pair.arrive()
+            for copy in self.forward:
+                copy.arrive()
+
+    class Reduce:
+        def __init__(self, part, pair_in, onward, chip_in, sems):
+            self.part, self.pair_in, self.onward, self.chip_in = part, pair_in, onward, chip_in
+            steps = ((0, 0),) + CHIPS
+            self.pair = [
+                Copy(
+                    part.at[member((dx, 1, dy))],
+                    pair_in.at[k],
+                    pair_in.at[k],
+                    sems,
+                    k,
+                    device(core),
+                )
+                for k, (dx, dy) in enumerate(steps)
+            ]
+            self.across = [
+                Copy(
+                    onward.at[k], chip_in.at[k], chip_in.at[k], sems, 4 + k, device((dx, 0, dy))
+                )
+                for k, (dx, dy) in enumerate(CHIPS)
+            ]
+
+        def start(self):
+            for k in (1, 2, 3, 0):
+                self.pair[k].start()
+
+        def middle(self):
+            for k, (dx, dy) in enumerate(CHIPS):
+                self.pair[k + 1].arrive()
+                total = self.part[member((dx, 0, dy))].astype(F32) + self.pair_in[k + 1].astype(F32)
+                self.onward[k] = total.astype(BF)
+                self.across[k].start()
+
+        def finish(self):
+            self.pair[0].arrive()
+            total = self.part[me].astype(F32) + self.pair_in[0].astype(F32)
+            for k in range(len(CHIPS)):
+                self.across[k].arrive()
+                total = total + self.chip_in[k].astype(F32)
+            return total
+
+    class Spread:
+        def __init__(self, source, target, sems):
+            self.source, self.target = source, target
+            self.copies = [
+                Copy(
+                    source.at[member(step)],
+                    target.at[me],
+                    target.at[member(step)],
+                    sems,
+                    k,
+                    device(step),
+                )
+                for k, step in enumerate(PLANE)
+            ]
+
+        def start(self):
+            for copy in self.copies:
+                copy.start()
+            self.target[me] = self.source[me]
+
+        def finish(self):
+            for copy in self.copies:
+                copy.arrive()
+
+    class Share:
+        def __init__(self, buffer, sems, block=None):
+            self.copies = [
+                Copy(
+                    buffer.at[me] if block is None else block,
+                    buffer.at[me],
+                    buffer.at[member(step)],
+                    sems,
+                    k,
+                    device(step),
+                )
+                for k, step in enumerate(PLANE)
+            ]
+
+        def start(self):
+            for copy in self.copies:
+                copy.start()
+
+        def finish(self):
+            for copy in self.copies:
+                copy.arrive()
+
+    class Line:
+        def __init__(self, buffer, sems, first=None):
+            self.copies = []
+            for along in range(1, lines):
+                back = (z + lines - along) % lines
+                if first is None:
+                    mine, theirs = buffer.at[z], buffer.at[back]
+                else:
+                    mine, theirs = buffer.at[pl.ds(first * z, first)], buffer.at[pl.ds(first * back, first)]
+                self.copies.append(Copy(mine, mine, theirs, sems, along - 1, device(here, along)))
+
+        def start(self):
+            for copy in self.copies:
+                copy.start()
+
+        def finish(self):
+            for copy in self.copies:
+                copy.arrive()
+
+    class Fold:
+        def __init__(self, terms, landed, sems):
+            self.terms, self.landed = terms, landed
+            self.copies = [
+                Copy(
+                    terms.at[(z + along) % lines],
+                    landed.at[along - 1],
+                    landed.at[along - 1],
+                    sems,
+                    along - 1,
+                    device(here, along),
+                )
+                for along in range(1, lines)
+            ]
+
+        def start(self):
+            for copy in self.copies:
+                copy.start()
+
+        def finish(self):
+            total = self.terms[z].astype(F32)
+            for k, copy in enumerate(self.copies):
+                copy.arrive()
+                total = total + self.landed[k].astype(F32)
+            return total
+
+    class Canvases:
+        def __init__(self, buffer, sems):
+            self.near = [
+                Copy(
+                    buffer.at[dp],
+                    buffer.at[dp],
+                    buffer.at[device(step)[0]],
+                    sems,
+                    k,
+                    device(step),
+                )
+                for k, step in enumerate(((1, 0, 0), (0, 1, 0), (1, 1, 0)))
+            ]
+            self.far = []
+            for along in range(1, lines):
+                back = (z + lines - along) % lines
+                mine = buffer.at[pl.ds(4 * z, 4)]
+                self.far.append(
+                    Copy(
+                        mine,
+                        mine,
+                        buffer.at[pl.ds(4 * back, 4)],
+                        sems,
+                        2 + along,
+                        device(here, along),
+                    )
+                )
+
+        def start(self):
+            for copy in self.near:
+                copy.start()
+
+        def middle(self):
+            for copy in self.near:
+                copy.arrive()
+            for copy in self.far:
+                copy.start()
+
+        def finish(self):
+            for copy in self.far:
+                copy.arrive()
+
+    def each_canvas(body, which=None):
+        if which is None:
+            lax.fori_loop(0, 4, lambda t, carry: (body(t), carry)[1], 0)
+        else:
+            base = c if which == 0 else 1 - c
+            lax.fori_loop(0, 2, lambda t, carry: (body(2 * t + base), carry)[1], 0)
+
+    def slots(t):
+        return pl.ds(2 * t, 2)
+
+    lane = lax.broadcasted_iota(jnp.int32, (1, lanes), 1)
+    first_head = lane < lanes // 2
+    first_part = (lane % 16) < 8
+
+    def per_head(pair):
+        return jnp.where(first_head, pair[0], pair[1])
+
+    def head_sums(value):
+        left = jnp.where(first_head, value, 0.0)
+        right = jnp.where(first_head, 0.0, value)
+        return (
+            jnp.sum(left, axis=-1, keepdims=True),
+            jnp.sum(right, axis=-1, keepdims=True),
+        )
+
+    def partner(value):
+        return jnp.where(
+            first_part, pltpu.roll(value, lanes - 8, 1), pltpu.roll(value, 8, 1)
+        )
+
+    ids = s.ids
+    ids[me] = jnp.zeros(ids.shape[1:], jnp.int32)
+    ids[me, 0:1, :] = crop_ref[...]
+    ids[me, 1:3, :] = pos_ref[0]
+    conds = s.conds
+    conds[dp] = jnp.zeros(conds.shape[1:], F32)
+    for r in range(cond_ref.shape[1] // 128):
+        conds[dp, r : r + 1, :] = cond_ref[:, 128 * r : 128 * (r + 1)].astype(F32)
+    s.tokens[me] = x_ref[...]
+    s.cots[me] = cot_ref[...]
+    s.out_line[z] = out_ref[...]
+    s.down_line[z] = down_ref[...]
+    mod_full = s.mod_full
+    mod_full[...] = jnp.zeros(mod_full.shape, BF)
+    mod_full[0:mod_rows, 0:width] = amod_ref[...]
+    mod_full[0:mod_rows, width : 2 * width] = fmod_ref[...]
+
+    barrier = pltpu.get_barrier_semaphore()
+    partners = [device(step) for step in PLANE] + [device(here, k) for k in range(1, lines)]
+    for target in partners:
+        pl.semaphore_signal(barrier, inc=1, device_id=target, device_id_type=MESH)
+    pl.semaphore_wait(barrier, len(partners))
+
+    cond_copy = Canvases(conds, s.sem_cond)
+    ids_copy = Share(ids, s.sem_ids)
+    qkv_spread = Spread(qkv_ref, s.qkv_line.at[z], s.sem_qkv_spread)
+    up_spread = Spread(up_ref, s.up_line.at[z], s.sem_up_spread)
+    qkv_line = Line(s.qkv_line, s.sem_qkv_line)
+    out_line = Line(s.out_line, s.sem_out_line)
+    up_line = Line(s.up_line, s.sem_up_line)
+    down_line = Line(s.down_line, s.sem_down_line)
+    token_copy = Gather(s.tokens, s.sem_tokens)
+    cot_copy = Gather(s.cots, s.sem_cots)
+    cond_copy.start()
+    qkv_spread.start()
+    ids_copy.start()
+    out_line.start()
+    token_copy.start()
+    cond_copy.middle()
+    qkv_spread.finish()
+    qkv_line.start()
+    up_spread.start()
+
+    cond_copy.finish()
+    picked = jnp.zeros((conds.shape[0], 128), F32)
+    for r in range(cond_ref.shape[1] // 128):
+        at_row = lax.broadcasted_iota(jnp.int32, (128, 128), 0) + 128 * r
+        at_col = lax.broadcasted_iota(jnp.int32, (128, 128), 1)
+        choose = (at_row == at_col + mod_rows * device_index) & (at_col < mod_rows)
+        picked = picked + dot(
+            conds[:, r, :].astype(BF), jnp.where(choose, 1.0, 0.0).astype(BF)
+        )
+    cond_mine = picked.astype(BF)
+    block_cols = 2 * width // 8
+    mod_terms, mod_in = s.mod_terms, s.mod_in
+    for m in range(8):
+        mod_terms[m] = dot(cond_mine, mod_full[:, block_cols * m : block_cols * (m + 1)])
+    mod_spread = Spread(mod_terms, mod_in, s.sem_mod_spread)
+    mod_spread.start()
+    token_copy.middle()
+    mod_spread.finish()
+    mod_sum = mod_in[0]
+    for m in range(1, 8):
+        mod_sum = mod_sum + mod_in[m]
+    mod_line = s.mod_line
+    mod_line[z] = mod_sum
+    mod_copy = Line(mod_line, s.sem_mod_line)
+    mod_copy.start()
+    up_spread.finish()
+    up_line.start()
+    down_line.start()
+    mod_copy.finish()
+    mod_sum = mod_line[0]
+    for k in range(1, lines):
+        mod_sum = mod_sum + mod_line[k]
+    s.mod_total[...] = 1.0 + mod_sum
+    mod_share = Share(s.mods, s.sem_mods)
+    own_rows = s.mod_total[pl.ds(8 * (z // 2), 8), :]
+    s.mods[me] = own_rows
+    mod_share.start()
+    token_copy.finish()
+    mod_share.finish()
+    scales = s.scales
+    for m in range(8):
+        scales[:, block_cols * m : block_cols * (m + 1)] = s.mods[m]
+    cot_copy.start()
+    ids_copy.finish()
+
+    def scale_row(canvas, ffn):
+        row = scales[pl.ds(4 * (z % 2) + canvas, 1), :]
+        return row[:, width:] if ffn else row[:, :width]
+
+    own_canvas = 2 * x + c
+
+    def inverse_rms(value):
+        return lax.rsqrt(jnp.mean(value * value, axis=-1, keepdims=True) + eps_norm)
+
+    normed = s.normed
+
+    def norm_tokens(canvas):
+        value = s.tokens[slots(canvas)].reshape(canvas_rows, width).astype(F32)
+        scaled = value * inverse_rms(value) * scale_row(canvas, False)
+        normed[slots(canvas)] = scaled.astype(BF).reshape(2, rows, width)
+
+    each_canvas(norm_tokens)
+    out_line.finish()
+    out_half = s.out_half
+    half_copy = Copy(
+        s.out_line.at[pl.ds(2 * (1 - y), 2)],
+        out_half,
+        out_half,
+        s.sem_half,
+        0,
+        device((0, 0, 1)),
+    )
+    half_copy.start()
+    qkv_line.finish()
+    head_of = lambda k: 8 * y + 4 * k + 2 * x + c
+    head_scales = [scale_ref[head_of(k)] for k in range(2)]
+    scale_lanes = per_head(head_scales)
+    root_lanes = jnp.sqrt(scale_lanes)
+
+    def canvas_ids(canvas, row):
+        return jnp.concatenate(
+            [ids[2 * canvas, row : row + 1, :], ids[2 * canvas + 1, row : row + 1, :]], axis=1
+        )
+
+    def one_hot(row, count):
+        return jnp.where(
+            lax.broadcasted_iota(jnp.int32, (count, canvas_rows), 0) == row, 1.0, 0.0
+        ).astype(BF)
+
+    def attend(canvas):
+        qkv = dot(
+            normed[slots(canvas)].reshape(canvas_rows, width),
+            s.qkv_line[...].reshape(width, own_cols),
+        )
+        places = [one_hot(canvas_ids(canvas, 1), 16), one_hot(canvas_ids(canvas, 2), 16)]
+        turn = dot(jnp.concatenate(places + places, axis=0), table_ref[me], 0, 0)
+        s.turns[canvas] = turn
+        cosine, sine = turn[:, :lanes], turn[:, lanes:]
+        rotated = []
+        for part in range(2):
+            raw = qkv[:, part * lanes : (part + 1) * lanes]
+            s.raw[canvas, part] = raw
+            sums = head_sums(raw * raw)
+            factor = per_head([lax.rsqrt(value + eps_cosine) for value in sums]) * root_lanes
+            turned = raw * factor
+            turned = (turned * cosine + partner(turned) * sine).astype(BF)
+            s.rotated[canvas, part] = turned
+            rotated.append(turned)
+        values = qkv[:, 2 * lanes :].astype(BF)
+        s.rotated[canvas, 2] = values
+        crop_hot = one_hot(canvas_ids(canvas, 0), crops)
+        allowed = dot(crop_hot, crop_hot, 0, 0)
+        heads = []
+        for k in range(2):
+            mine = first_head if k == 0 else jnp.logical_not(first_head)
+            query = jnp.where(mine, rotated[0], jnp.zeros_like(rotated[0]))
+            weights = jnp.exp(dot(query, rotated[1], 1, 1)) * allowed
+            probs = weights / jnp.sum(weights, axis=-1, keepdims=True)
+            s.probs[canvas, k] = probs
+            heads.append(dot(probs.astype(BF), values))
+        attended = per_head(heads)
+        s.raw_attended[canvas] = attended
+        s.attended[canvas] = attended.astype(BF)
+
+    each_canvas(attend)
+    half_copy.arrive()
+    out_full = s.out_full
+    for k in range(2):
+        out_full[k, y] = s.out_line[2 * y + k]
+        out_full[k, 1 - y] = out_half[k]
+
+    def to_middle(canvas):
+        value = dot(s.attended[canvas], out_full[...].reshape(lanes, width))
+        s.mid_part[slots(canvas)] = value.astype(BF).reshape(2, rows, width)
+
+    mid_reduce = Reduce(
+        s.mid_part, s.mid_pair, s.mid_onward, s.mid_chip, s.sem_mid
+    )
+    each_canvas(to_middle, 1)
+    mid_reduce.start()
+    each_canvas(to_middle, 0)
+    mid_reduce.middle()
+    cot_copy.middle()
+    middle = x_ref[...].astype(F32) + mid_reduce.finish()
+    s.middle[...] = middle
+    ffn_row = scale_row(own_canvas, True)
+    s.ffn[me] = (middle * inverse_rms(middle) * ffn_row).astype(BF)
+    ffn_copy = Gather(s.ffn, s.sem_ffn)
+    ffn_copy.start()
+    cot_copy.finish()
+    up_line.finish()
+
+    def feed(canvas):
+        up = dot(
+            s.ffn[slots(canvas)].reshape(canvas_rows, width),
+            s.up_line[...].reshape(width, 2 * hidden),
+        )
+        value, gate = up[:, :hidden], up[:, hidden:]
+        cdf = 0.5 + 0.5 * erf(gate * math.sqrt(0.5))
+        act = gate * cdf
+        s.hidden[canvas] = (value * act).astype(BF)
+        s.act[canvas] = act
+        density = jnp.exp(-0.5 * gate * gate) * (1.0 / math.sqrt(2.0 * math.pi))
+        s.slope[canvas] = value * (cdf + gate * density)
+
+    ffn_copy.middle()
+    each_canvas(feed, 0)
+    ffn_copy.finish()
+    each_canvas(feed, 1)
+
+    def cots_of(canvas):
+        return s.cots[slots(canvas)].reshape(canvas_rows, width)
+
+    all_rows = 8 * rows
+    chunk = 256
+
+    def down_term(n, carry):
+        cols = pl.ds(pl.multiple_of(n * chunk, chunk), chunk)
+        term = dot(
+            s.hidden[...].reshape(all_rows, hidden),
+            s.cots[:, :, cols].reshape(all_rows, chunk),
+            0,
+            0,
+        )
+        s.down_term[:, :, cols] = term.astype(BF).reshape(lines, down_rows, chunk)
+        return carry
+
+    lax.fori_loop(0, width // chunk, down_term, 0)
+    down_fold = Fold(s.down_term, s.down_in, s.sem_down_fold)
+    down_fold.start()
+    down_line.finish()
+
+    def feed_back(canvas):
+        grad_hidden = dot(cots_of(canvas), s.down_line[...].reshape(hidden, width), 1, 1)
+        grad_up = jnp.concatenate(
+            [grad_hidden * s.act[canvas], grad_hidden * s.slope[canvas]], axis=1
+        ).astype(BF)
+        s.grad_up[canvas] = grad_up
+        part = dot(grad_up, s.up_line[...].reshape(width, 2 * hidden), 1, 1)
+        s.gnf_part[slots(canvas)] = part.astype(BF).reshape(2, rows, width)
+
+    gnf_reduce = Reduce(
+        s.gnf_part, s.gnf_pair, s.gnf_onward, s.gnf_chip, s.sem_gnf
+    )
+    each_canvas(feed_back, 1)
+    gnf_reduce.start()
+    each_canvas(feed_back, 0)
+    gnf_reduce.middle()
+
+    def up_term(k, carry):
+        cols = pl.ds(pl.multiple_of(k * 8 * up_rows, 8 * up_rows), 8 * up_rows)
+        term = dot(
+            s.ffn[:, :, cols].reshape(all_rows, 8 * up_rows),
+            s.grad_up[...].reshape(all_rows, 2 * hidden),
+            0,
+            0,
+        )
+        s.up_term[k] = term.astype(BF).reshape(8, up_rows, 2 * hidden)
+        return carry
+
+    lax.fori_loop(0, lines, up_term, 0)
+    up_fold = Fold(s.up_term, s.up_in, s.sem_up_fold)
+    up_fold.start()
+
+    def norm_back(value, row, grad):
+        inverse = inverse_rms(value)
+        scaled = grad * row
+        along = jnp.mean(scaled * value, axis=-1, keepdims=True)
+        grad_value = inverse * scaled - value * (inverse * inverse * inverse) * along
+        return grad_value, jnp.sum(grad * value * inverse, axis=0, keepdims=True)
+
+    def put_row(target, offset, row):
+        for r in range(width // 128):
+            target[offset + r : offset + r + 1, :] = row[:, 128 * r : 128 * (r + 1)]
+
+    grad_mid, ffn_sum = norm_back(s.middle[...], ffn_row, gnf_reduce.finish())
+    grad_middle = cot_ref[...].astype(F32) + grad_mid
+    s.grad_middle[...] = grad_middle
+    s.branch[me] = grad_middle.astype(BF)
+    branch_copy = Gather(s.branch, s.sem_branch)
+    branch_copy.start()
+    sums_own = s.sums_own
+    put_row(sums_own, 8, ffn_sum)
+
+    def to_out(canvas):
+        part = dot(s.hidden[canvas], s.down_line[...].reshape(hidden, width))
+        s.out_part[slots(canvas)] = part.astype(BF).reshape(2, rows, width)
+
+    out_reduce = Reduce(
+        s.out_part, s.out_pair, s.out_onward, s.out_chip, s.sem_out
+    )
+    each_canvas(to_out)
+    branch_copy.middle()
+    out_reduce.start()
+
+    def attend_back(canvas):
+        branch = s.branch[slots(canvas)].reshape(canvas_rows, width)
+        grad_att = dot(branch, out_full[...].reshape(lanes, width), 1, 1).astype(BF)
+        turn = s.turns[canvas]
+        cosine, sine = turn[:, :lanes], turn[:, lanes:]
+        query, key, values = (s.rotated[canvas, part] for part in range(3))
+        deltas = head_sums(grad_att.astype(F32) * s.raw_attended[canvas])
+        grads = [[], [], []]
+        for k in range(2):
+            mine = first_head if k == 0 else jnp.logical_not(first_head)
+            probs = s.probs[canvas, k]
+            one_head = jnp.where(mine, grad_att, jnp.zeros_like(grad_att))
+            dotted = dot(one_head, values, 1, 1)
+            slope = (probs * (dotted - deltas[k])).astype(BF)
+            grads[0].append(dot(slope, key))
+            grads[1].append(dot(slope, query, 0, 0))
+            grads[2].append(dot(probs.astype(BF), grad_att, 0, 0))
+        pieces = []
+        for part in range(2):
+            grad = per_head(grads[part])
+            grad = grad * cosine - partner(grad) * sine
+            raw = s.raw[canvas, part]
+            squares = [value + eps_cosine for value in head_sums(raw * raw)]
+            along = head_sums(grad * raw)
+            inverse = [lax.rsqrt(value) for value in squares]
+            factor = per_head(inverse) * root_lanes
+            shrink = per_head([along[k] * inverse[k] * inverse[k] for k in range(2)])
+            pieces.append(factor * grad - raw * factor * shrink)
+            term = per_head([jnp.sum(along[k] * inverse[k], axis=0, keepdims=True) for k in range(2)])
+            s.head_terms[...] += term * root_lanes / (2.0 * scale_lanes)
+        pieces.append(per_head(grads[2]))
+        grad_qkv = jnp.concatenate(pieces, axis=1).astype(BF)
+        s.grad_qkv[canvas] = grad_qkv
+        part = dot(grad_qkv, s.qkv_line[...].reshape(width, own_cols), 1, 1)
+        s.gna_part[slots(canvas)] = part.astype(BF).reshape(2, rows, width)
+
+    s.head_terms[...] = jnp.zeros((1, lanes), F32)
+    branch_copy.finish()
+    gna_reduce = Reduce(
+        s.gna_part, s.gna_pair, s.gna_onward, s.gna_chip, s.sem_gna
+    )
+    each_canvas(attend_back, 1)
+    gna_reduce.start()
+    each_canvas(attend_back, 0)
+    gna_reduce.middle()
+
+    def qkv_term(k, carry):
+        cols = pl.ds(pl.multiple_of(k * 8 * up_rows, 8 * up_rows), 8 * up_rows)
+        term = dot(
+            normed[:, :, cols].reshape(all_rows, 8 * up_rows),
+            s.grad_qkv[...].reshape(all_rows, own_cols),
+            0,
+            0,
+        )
+        s.qkv_term[k] = term.astype(BF).reshape(8, up_rows, own_cols)
+        return carry
+
+    lax.fori_loop(0, lines, qkv_term, 0)
+    qkv_fold = Fold(s.qkv_term, s.qkv_in, s.sem_qkv_fold)
+    qkv_fold.start()
+
+    term = dot(
+        s.attended[...].reshape(all_rows, lanes),
+        s.branch[...].reshape(all_rows, width),
+        0,
+        0,
+    ).astype(BF).reshape(2, 2, half_head, width)
+    halves = s.out_halves
+    for k in range(2):
+        for half in range(2):
+            halves[half, k] = term[k, half]
+    swap = Copy(
+        halves.at[1 - y], s.out_swap, s.out_swap, s.sem_half, 1, device((0, 0, 1))
+    )
+    swap.start()
+
+    grad_in, attn_sum = norm_back(x_ref[...].astype(F32), scale_row(own_canvas, False), gna_reduce.finish())
+    input_grad[...] = s.grad_middle[...] + grad_in
+    put_row(sums_own, 0, attn_sum)
+    head_rows = lax.broadcasted_iota(jnp.int32, (8, lanes), 0)
+    head_lane = lax.broadcasted_iota(jnp.int32, (8, lanes), 1)
+    head_tile = jnp.zeros((8, lanes), F32)
+    for k in range(2):
+        value = jnp.sum(
+            jnp.where(lane == k * (lanes // 2), s.head_terms[...], 0.0), axis=1, keepdims=True
+        )
+        head_tile = head_tile + jnp.where(
+            (head_rows == 0) & (head_lane == head_of(k)), value, 0.0
+        )
+    sums_own[16:24, :] = head_tile
+    sums_copy = Copy(
+        sums_own, s.sums_pair, s.sums_pair, s.sem_half, 2, device((0, 0, 1))
+    )
+    sums_copy.start()
+    out_reduce.middle()
+    swap.arrive()
+    out_terms = s.out_terms
+    for k in range(2):
+        out_terms[2 * y + k] = halves[y, k]
+        out_terms[2 * (1 - y) + k] = s.out_swap[k]
+    out_fold = Fold(out_terms, s.out_in, s.sem_out_fold)
+    out_fold.start()
+    sums_copy.arrive()
+    sums = s.sums
+    sums[dp] = sums_own[...] + s.sums_pair[...]
+    all_sums = Canvases(sums, s.sem_sums)
+    all_sums.start()
+    down_grad[...] = down_fold.finish().reshape(down_rows, width)
+    all_sums.middle()
+    block_out[...] = (s.middle[...] + out_reduce.finish()).astype(BF)
+    s.up_sum[...] = up_fold.finish().astype(BF)
+    up_return = Spread(s.up_sum, s.up_back, s.sem_up_back)
+    up_return.start()
+    s.qkv_sum[...] = qkv_fold.finish().astype(BF)
+    qkv_return = Spread(s.qkv_sum, s.qkv_back, s.sem_qkv_back)
+    qkv_return.start()
+
+    all_sums.finish()
+    rounded = [
+        jnp.concatenate([sums[:, offset + r, :] for r in range(width // 128)], axis=1).astype(BF)
+        for offset in (0, 8)
+    ]
+    mine_for = dot(rounded[0], mod_full[:, :width], 1, 1) + dot(
+        rounded[1], mod_full[:, width:], 1, 1
+    )
+    cond_line, cond_in = s.cond_line, s.cond_in
+    s.cond_all[...] = mine_for
+    for k in range(lines):
+        cond_line[k] = s.cond_all[8 * (k // 2) : 8 * (k // 2) + 8, :]
+    cond_send = [
+        Copy(
+            cond_line.at[(z + along) % lines],
+            cond_in.at[me, z],
+            cond_in.at[me, (z + lines - along) % lines],
+            s.sem_cond_line,
+            along - 1,
+            device(here, along),
+        )
+        for along in range(1, lines)
+    ]
+    for copy in cond_send:
+        copy.start()
+    cond_in[me, z] = cond_line[z]
+    amod_grad[...] = dot(cond_mine, rounded[0], 0, 0)[:mod_rows]
+    fmod_grad[...] = dot(cond_mine, rounded[1], 0, 0)[:mod_rows]
+    head_sum = sums[0, 16:17, :]
+    for k in range(1, sums.shape[0]):
+        head_sum = head_sum + sums[k, 16:17, :]
+    scale_grad[...] = head_sum
+    for copy in cond_send:
+        copy.arrive()
+    cond_share = Share(cond_in, s.sem_cond_share)
+    cond_share.start()
+    out_grad[...] = out_fold.finish()
+    cond_share.finish()
+    for k in range(lines):
+        for m in range(8):
+            at_row = 8 * k + m
+            cond_grad[at_row : at_row + 1, :] = cond_in[m, k, pl.ds(4 * (z % 2) + own_canvas, 1), :]
+    up_return.finish()
+    up_grad[...] = s.up_back[...]
+    qkv_return.finish()
+    qkv_grad[...] = s.qkv_back[...]
+    for copy in sends:
+        copy.wait_send()
+
+
+def scratch_plan(lines, x_ref, qkv_ref, up_ref, out_ref, down_ref):
+    rows, width = x_ref.shape
+    own_cols = qkv_ref.shape[2]
+    up_rows, up_cols = up_ref.shape[1:]
+    hidden = up_cols // 2
+    half_head = out_ref.shape[0]
+    down_rows = down_ref.shape[0]
+    lanes = own_cols // 3
+    groups = 4 * lines
+    plane = (8, rows, width)
+    vm = lambda shape, kind=BF: pltpu.VMEM(shape, kind)
+    sem = lambda count: pltpu.SemaphoreType.DMA((2, count))
+    plan = dict(
+        ids=vm((8, 8, rows), jnp.int32),
+        conds=vm((groups, 8, 128), F32),
+        tokens=vm(plane),
+        cots=vm(plane),
+        normed=vm(plane),
+        ffn=vm(plane),
+        branch=vm(plane),
+        qkv_line=vm((lines, 8, up_rows, own_cols)),
+        up_line=vm((lines, 8, up_rows, up_cols)),
+        out_line=vm((lines, half_head, width)),
+        down_line=vm((lines, down_rows, width)),
+        out_half=vm((2, half_head, width)),
+        out_full=vm((2, 2, half_head, width)),
+        mod_full=vm((128, 2 * width)),
+        mod_terms=vm((8, groups, width // 4), F32),
+        mod_in=vm((8, groups, width // 4), F32),
+        mod_line=vm((lines, groups, width // 4), F32),
+        mod_total=vm((groups, width // 4), F32),
+        mods=vm((8, 8, width // 4), F32),
+        scales=vm((8, 2 * width), F32),
+        turns=vm((4, 2 * rows, 2 * lanes), F32),
+        raw=vm((4, 2, 2 * rows, lanes), F32),
+        rotated=vm((4, 3, 2 * rows, lanes)),
+        probs=vm((4, 2, 2 * rows, 2 * rows), F32),
+        raw_attended=vm((4, 2 * rows, lanes), F32),
+        attended=vm((4, 2 * rows, lanes)),
+        middle=vm((rows, width), F32),
+        grad_middle=vm((rows, width), F32),
+        hidden=vm((4, 2 * rows, hidden)),
+        act=vm((4, 2 * rows, hidden), F32),
+        slope=vm((4, 2 * rows, hidden), F32),
+        grad_up=vm((4, 2 * rows, up_cols)),
+        grad_qkv=vm((4, 2 * rows, own_cols)),
+        head_terms=vm((1, lanes), F32),
+        sums_own=vm((24, 128), F32),
+        sums_pair=vm((24, 128), F32),
+        sums=vm((groups, 24, 128), F32),
+        cond_all=vm((groups, 128), F32),
+        cond_line=vm((lines, 8, 128), F32),
+        cond_in=vm((8, lines, 8, 128), F32),
+        down_term=vm((lines, down_rows, width)),
+        down_in=vm((lines - 1, down_rows, width)),
+        up_term=vm((lines, 8, up_rows, up_cols)),
+        up_in=vm((lines - 1, 8, up_rows, up_cols)),
+        up_sum=vm((8, up_rows, up_cols)),
+        up_back=vm((8, up_rows, up_cols)),
+        qkv_term=vm((lines, 8, up_rows, own_cols)),
+        qkv_in=vm((lines - 1, 8, up_rows, own_cols)),
+        qkv_sum=vm((8, up_rows, own_cols)),
+        qkv_back=vm((8, up_rows, own_cols)),
+        out_halves=vm((2, 2, half_head, width)),
+        out_swap=vm((2, half_head, width)),
+        out_terms=vm((lines, half_head, width)),
+        out_in=vm((lines - 1, half_head, width)),
+    )
+    for name in ("mid", "gnf", "out", "gna"):
+        plan[name + "_part"] = vm(plane)
+        plan[name + "_pair"] = vm((4, rows, width))
+        plan[name + "_onward"] = vm((3, rows, width))
+        plan[name + "_chip"] = vm((3, rows, width))
+        plan["sem_" + name] = sem(7)
+    plan.update(
+        sem_tokens=sem(7),
+        sem_cots=sem(7),
+        sem_ffn=sem(7),
+        sem_branch=sem(7),
+        sem_ids=sem(7),
+        sem_qkv_spread=sem(7),
+        sem_up_spread=sem(7),
+        sem_mod_spread=sem(7),
+        sem_mods=sem(7),
+        sem_up_back=sem(7),
+        sem_qkv_back=sem(7),
+        sem_cond_share=sem(7),
+        sem_qkv_line=sem(lines - 1),
+        sem_up_line=sem(lines - 1),
+        sem_out_line=sem(lines - 1),
+        sem_down_line=sem(lines - 1),
+        sem_mod_line=sem(lines - 1),
+        sem_cond_line=sem(lines - 1),
+        sem_down_fold=sem(lines - 1),
+        sem_up_fold=sem(lines - 1),
+        sem_qkv_fold=sem(lines - 1),
+        sem_out_fold=sem(lines - 1),
+        sem_cond=sem(lines + 2),
+        sem_sums=sem(lines + 2),
+        sem_half=sem(3),
+    )
+    return plan
+
+
+def turn_tables(heads, lines):
+    head_size = 64
+    table = np.zeros((heads, 2, 16, 2, head_size), np.float64)
+    for axis in range(2):
+        for j in range(8):
+            freq = math.pi * 10.0 ** ((j * heads + np.arange(heads)) / (8.0 * heads))
+            unit = (2.0 * np.arange(16) + 1.0) / 16.0 - 1.0
+            angle = freq[:, None].astype(np.float32) * unit[None, :].astype(np.float32)
+            angle = angle.astype(np.float64)
+            for half in range(2):
+                at = axis * 16 + half * 8 + j
+                table[:, axis, :, 0, at] = np.cos(angle)
+                table[:, axis, :, 1, at] = np.sin(angle) * (1.0 if half else -1.0)
+    table[:, 0, :, 0, 32:] = 1.0
+    high = table.astype(ml_dtypes.bfloat16)
+    low = (table - high.astype(np.float64)).astype(ml_dtypes.bfloat16)
+    parts = []
+    for term in (high, low):
+        term = term.reshape(2, 2, 2, 2, 2, 16, 2, head_size)
+        term = term.transpose(2, 3, 0, 4, 5, 6, 1, 7)
+        parts.append(term.reshape(8, 32, 4 * head_size))
+    return np.concatenate(parts, axis=1)
+
+
+def plane_shards(
+    block_in,
+    conditioning,
+    crop_ids,
+    positions,
+    qkv_weight,
+    out_weight,
+    up_weight,
+    down_weight,
+    attn_modulate,
+    ffn_modulate,
+    head_scale,
+    cotangent,
+):
+    lines = lax.axis_size("dp") // 4
+    rows, width = block_in.shape[1:]
+    heads = head_scale.shape[0]
+    up_rows = qkv_weight.shape[0]
+    own_hidden = down_weight.shape[0]
+    qkv = qkv_weight.reshape(up_rows, 3, 2, 2, 2, 2, 64).transpose(4, 5, 2, 0, 1, 3, 6)
+    qkv = qkv.reshape(8, up_rows, -1)
+    up = up_weight.reshape(up_rows, 2, lines, 8, own_hidden).transpose(3, 0, 1, 2, 4)
+    up = up.reshape(8, up_rows, -1)
+    tables = jnp.asarray(turn_tables(heads, lines))
+    kinds = jax.ShapeDtypeStruct
+    operands = (
+        block_in[0],
+        cotangent[0],
+        qkv,
+        up,
+        out_weight,
+        down_weight,
+        attn_modulate,
+        ffn_modulate,
+        conditioning,
+        crop_ids,
+        positions,
+        head_scale,
+        tables,
+    )
+    plan = scratch_plan(lines, operands[0], qkv, up, out_weight, down_weight)
+    in_vmem = pl.BlockSpec(memory_space=pltpu.VMEM)
+    in_specs = [in_vmem] * len(operands)
+    in_specs[11] = pl.BlockSpec(memory_space=pltpu.SMEM)
+    results = pl.pallas_call(
+        functools.partial(block_kernel, lines),
+        out_shape=(
+            kinds((rows, width), BF),
+            kinds((rows, width), F32),
+            kinds((8 * lines, 128), F32),
+            kinds(qkv.shape, BF),
+            kinds(out_weight.shape, F32),
+            kinds(up.shape, BF),
+            kinds(down_weight.shape, F32),
+            kinds(attn_modulate.shape, F32),
+            kinds(ffn_modulate.shape, F32),
+            kinds((1, 128), F32),
+        ),
+        in_specs=in_specs,
+        out_specs=[in_vmem] * 10,
+        scratch_shapes=list(plan.values()),
+        compiler_params=pltpu.CompilerParams(
+            collective_id=0, has_side_effects=True, vmem_limit_bytes=63 * 2**20
+        ),
+    )(*operands)
+    block_out, input_grad, cond, qkv_back, out_grad, up_back, down_grad, amod, fmod, scale = results
+    mod_rows = attn_modulate.shape[0]
+    cond_grad = cond[:, :mod_rows].reshape(1, -1)
+    qkv_grad = qkv_back.reshape(2, 2, 2, up_rows, 3, 2, 64).transpose(3, 4, 2, 5, 0, 1, 6)
+    qkv_grad = qkv_grad.reshape(qkv_weight.shape).astype(F32)
+    up_grad = up_back.reshape(8, up_rows, 2, lines, own_hidden).transpose(1, 2, 3, 0, 4)
+    up_grad = up_grad.reshape(up_weight.shape).astype(F32)
+    return (
+        block_out[None],
+        input_grad[None],
+        cond_grad,
+        qkv_grad,
+        out_grad,
+        up_grad,
+        down_grad,
+        amod,
+        fmod,
+        scale[0, :heads],
+    )
+
+
+def in_planes(mesh):
+    return mesh.shape["seq"] == 2 and mesh.shape["dp"] == 16
+
+
 def solution(mesh):
     in_specs = (
         P("dp", "seq", None),
@@ -346,4 +1395,5 @@
         P(("dp", "seq"), None),
         P(),
     )
-    return jax.shard_map(shards, mesh=mesh, in_specs=in_specs, out_specs=out_specs, check_vma=False)
+    body = plane_shards if in_planes(mesh) else shards
+    return jax.shard_map(body, mesh=mesh, in_specs=in_specs, out_specs=out_specs, check_vma=False)

time: 1500 us -> 214 us (0.14)
  waiting for transfers between devices: 1160 us -> 0 us
  Pallas kernels: 0 us -> 196 us
  local copies, waits for them, and re-layouts: 150 us -> 17 us
  matrix products: 74.8 us -> 0 us
  blocking collectives: 72.7 us -> 0 us
  other arithmetic: 20.4 us -> 0 us
    unnamed x10 -> x0, waiting for transfers between devices: 809 us -> none
    all_gather x6 -> x0, waiting for transfers between devices: 353 us -> none  [the longest x1 91.2 us: shards(): lax.all_gather(up_weight, ('dp', 'seq'), axis=0, tiled=True)]
    pallas_call x0 -> x1, Pallas kernels: none -> 196 us  [plane_shards(): pl.pallas_call(functools.partial(block_kernel, lines), out_shape=(kinds((...]
    dot_general x22 -> x0, matrix products: 74.8 us -> none  [the longest x1 10.3 us: shards(): jnp.einsum('csd,cse->de', normed_ffn, grad_up, preferred_element_type=jnp...]
    reshape x12 -> x7, local copies, waits for them, and re-layouts: 62.1 us -> 5.08 us  [the longest x2 1.72 us: plane_shards(): up_weight.reshape(up_rows, 2, lines, 8, own_hidden).transpose(3, 0, 1, 2, 4)]
    unnamed x118 -> x26, local copies, waits for them, and re-layouts: 55.5 us -> 4.92 us
    psum x2 -> x0, blocking collectives: 49 us -> none  [the longest x1 40.2 us: shards(): scale_grad = lax.psum(scale_local, ('dp', 'seq'))]
    all_gather x3 -> x0, blocking collectives: 23.8 us -> none  [the longest x1 9.26 us: shards(): piece_values = lax.all_gather(values_flat, 'seq', axis=1, tiled=True)]
  transfers between devices with their start and end apart: 8 -> 0, of which waited for: 7 -> 0; matrix products, arithmetic and copies ran while one was open for 7% -> 0% of each run, Pallas kernels for 0% -> 0%
where the time goes in v1:
time: 214 us
  Pallas kernels  196 us (92%)
  local copies, waits for them, and re-layouts  17 us (8%)
    pallas_call x1, Pallas kernels, plane_shards(): pl.pallas_call(functools.partial(block_kernel, lines), out_shape=(kinds((...  196 us
    unnamed x26, local copies, waits for them, and re-layouts  4.92 us

profile of v1, /device:TPU:0, one launch (start us, length us, event | category | flops | bytes accessed | tf_op | source)
XLA Modules:
  0.0 214.0 jit_solution(3206469309781798004)
XLA Ops:
  0.6 1.5 reshape.49
  2.2 0.2 copy.33
  2.4 0.0 copy-start.3
  2.4 1.2 reshape.50.up_ref
  3.6 0.0 copy-done.3
  3.6 0.3 reshape.47
  3.8 0.3 copy.34
  4.1 0.9 reshape.48.qkv_ref
  5.1 196.2 %shard_map.204 = (bf16[128,1024]{1,0:T(8,128)(2,1)}, f32[128,1024]{1,0:T(8,128)}, f32[32,128]{1,0:T(8,128)}, bf16[8,32,384]{2,1,0:T(8,128)(2,1)}, f32[32,1024]{1...) custom-call(bf16[128,1024]{1,0:T(8,128)(2,1)} %bitcast.23, ...), custom_call_target="tpu_custom_call" | custom-call | tf_op jit(solution)/shard_map/pallas_call | solution.py:1325
  201.3 1.8 reshape.55
  203.2 0.6 copy.30
  203.8 0.0 copy-start.4
  203.8 1.5 reshape.53
  205.3 0.0 copy-done.4
  205.3 0.5 reshape.54
  205.8 0.6 copy.29
  206.5 0.0 copy-start.8
  206.5 0.0 copy-start.9
  206.5 0.0 copy-start.2
  206.5 1.4 reshape.52
  207.9 0.0 copy-start
  207.9 0.0 copy-done.8
  207.9 0.7 reshape.51
  208.6 0.0 copy-done.9
  208.6 0.5 slice_bitcast_fusion
  209.1 0.0 copy-done.2
  209.1 0.7 copy.41
  209.8 0.0 copy-done
  209.8 0.0 copy-start.5
  209.8 0.0 copy-start.1
  209.8 0.8 copy.42
  210.6 0.2 copy-done.5
  210.8 0.7 copy.43
  211.5 0.0 copy-done.1
  211.5 0.0 copy-start.7
  211.5 0.7 copy.44
  212.2 0.2 copy-done.7
  212.4 0.0 copy-start.6
  212.4 0.6 copy.45
  213.1 0.3 copy-done.6
  213.4 0.6 copy.46
Async XLA Ops:
  2.4 1.2 copy-start.3
  203.8 1.5 copy-start.4
  206.5 1.5 copy-start.8
  206.5 2.1 copy-start.9
  206.5 2.6 %copy-start.2 = (bf16[128,1024]{1,0:T(8,128)(2,1)S(1)}, bf16[128,1024]{1,0:T(8,128)(2,1)}, u32[]{:S(2)}) copy-start(bf16[128,1024]{1,0:T(8,128)(2,1)} %get-tuple-element.20) | copy-start | bytes 786436
  207.9 1.9 copy-start
  209.8 1.0 copy-start.5
  209.8 1.7 copy-start.1
  211.5 1.0 copy-start.7
  212.4 0.9 copy-start.6

commit v2 on v1

--- a/solution.py
+++ b/solution.py
@@ -329,7 +329,7 @@
 BF = jnp.bfloat16
 F32 = jnp.float32
 PLANE = ((1, 0, 0), (0, 0, 1), (1, 0, 1), (0, 1, 0), (1, 1, 0), (0, 1, 1), (1, 1, 1))
-CHIPS = ((1, 0), (0, 1), (1, 1))
+TO_X, TO_Y, TO_FAR = (1, 0, 0), (0, 0, 1), (1, 0, 1)
 ERF_P = (
     0.00022905065861350646,
     0.0034082910107109506,
@@ -401,12 +401,12 @@
     x = (dp // 2) % 2
     c = dp % 2
     rows, width = x_ref.shape
-    own_cols = qkv_ref.shape[2]
+    up_rows = up_ref.shape[0]
+    own_cols = qkv_ref.shape[1] // 8
     lanes = own_cols // 3
     half_head = out_ref.shape[0]
-    hidden = up_ref.shape[2] // 2
+    hidden = up_ref.shape[1] // 16
     down_rows = down_ref.shape[0]
-    up_rows = up_ref.shape[1]
     mod_rows = amod_ref.shape[0]
     canvas_rows = 2 * rows
     crops = canvas_rows // 16
@@ -421,6 +421,12 @@
             ((z + along) % lines) * 4 + ((x + step[0]) % 2) * 2 + (c + step[1]) % 2,
             (y + step[2]) % 2,
         )
+
+    def line_device(along):
+        return (jnp.clip(z + along, 0, lines - 1) * 4 + dp % 4, y)
+
+    def inside(along):
+        return z + along < lines if along > 0 else z + along >= 0
 
     here = (0, 0, 0)
     core = (0, 1, 0)
@@ -445,82 +451,157 @@
                 device_id_type=MESH,
             )
 
-        def start(self):
-            self.out.start()
-            sends.append(self.out)
+        def start(self, when=None):
+            if when is None:
+                self.out.start()
+            else:
+                pl.when(when)(self.out.start)
+            sends.append((self.out, when))
 
         def arrive(self):
             self.into.wait_recv()
 
     class Gather:
         def __init__(self, buffer, sems):
-            self.buffer = buffer
             at = lambda step: buffer.at[member(step)]
-            self.across = [
-                Copy(at(here), at(here), at((dx, 0, dy)), sems, k, device((dx, 0, dy)))
-                for k, (dx, dy) in enumerate(CHIPS)
+            half = buffer.shape[1] // 2
+            rows_of = (pl.ds(0, half), pl.ds(half, half))
+            part = lambda step, k: buffer.at[member(step), rows_of[k]]
+            self.x_own = [
+                Copy(part(here, k), part(here, k), part(TO_X, k), sems, k, device(TO_X))
+                for k in range(2)
             ]
-            self.pair = Copy(at(here), at(here), at(core), sems, 3, device(core))
-            self.forward = [
-                Copy(at((dx, 0, dy)), at((dx, 0, dy)), at((dx, 1, dy)), sems, 4 + k, device(core))
-                for k, (dx, dy) in enumerate(CHIPS)
+            self.y_own = [
+                Copy(part(here, k), part(here, k), part(TO_Y, k), sems, 2 + k, device(TO_Y))
+                for k in range(2)
             ]
+            self.y_far = Copy(part(TO_X, 0), part(TO_X, 0), part(TO_FAR, 0), sems, 4, device(TO_Y))
+            self.x_far = Copy(part(TO_Y, 1), part(TO_Y, 1), part(TO_FAR, 1), sems, 5, device(TO_X))
+            self.pair = Copy(at(here), at(here), at(core), sems, 6, device(core))
+            self.cross = [
+                Copy(at(step), at(step), at((step[0], 1, step[2])), sems, 7 + k, device(core))
+                for k, step in enumerate((TO_X, TO_Y, TO_FAR))
+            ]
 
         def start(self):
-            for copy in self.across:
-                copy.start()
+            self.x_own[0].start()
+            self.y_own[1].start()
+            self.x_own[1].start()
+            self.y_own[0].start()
             self.pair.start()
 
-        def middle(self):
-            for copy, onward in zip(self.across, self.forward):
-                copy.arrive()
-                onward.start()
+        def turn(self):
+            self.x_own[0].arrive()
+            self.y_far.start()
+            self.y_own[1].arrive()
+            self.x_far.start()
+
+        def near(self):
+            self.y_own[0].arrive()
+            self.cross[1].start()
+            self.x_own[1].arrive()
+            self.cross[0].start()
+
+        def far(self):
+            self.y_far.arrive()
+            self.x_far.arrive()
+            self.cross[2].start()
+
+        def pair_near(self):
+            self.pair.arrive()
+            self.cross[1].arrive()
+
+        def pair_far(self):
+            self.cross[0].arrive()
+            self.cross[2].arrive()
 
         def finish(self):
-            self.pair.arrive()
-            for copy in self.forward:
-                copy.arrive()
+            self.near()
+            self.far()
+            self.pair_near()
+            self.pair_far()
+
+        def steps(self):
+            return {0: self.near, 1: self.pair_near, 2: self.far, 3: self.pair_far}
 
     class Reduce:
-        def __init__(self, part, pair_in, onward, chip_in, sems):
-            self.part, self.pair_in, self.onward, self.chip_in = part, pair_in, onward, chip_in
-            steps = ((0, 0),) + CHIPS
+        def __init__(self, part, pair_in, far_in, chip_in, sems):
+            self.part, self.pair_in, self.far_in, self.chip_in = part, pair_in, far_in, chip_in
+            half = part.shape[1] // 2
+            self.rows_of = rows_of = (pl.ds(0, half), pl.ds(half, half))
+            self.steps_of = (here, TO_X, TO_Y, TO_FAR)
             self.pair = [
                 Copy(
-                    part.at[member((dx, 1, dy))],
+                    part.at[member((step[0], 1, step[2]))],
                     pair_in.at[k],
                     pair_in.at[k],
                     sems,
                     k,
                     device(core),
                 )
-                for k, (dx, dy) in enumerate(steps)
+                for k, step in enumerate(self.steps_of)
             ]
-            self.across = [
-                Copy(
-                    onward.at[k], chip_in.at[k], chip_in.at[k], sems, 4 + k, device((dx, 0, dy))
-                )
-                for k, (dx, dy) in enumerate(CHIPS)
+            piece = lambda step, k: part.at[member(step), rows_of[k]]
+            self.x_far = Copy(piece(TO_FAR, 0), far_in.at[0], far_in.at[0], sems, 4, device(TO_X))
+            self.y_far = Copy(piece(TO_FAR, 1), far_in.at[1], far_in.at[1], sems, 5, device(TO_Y))
+            into = lambda way, k: chip_in.at[way, rows_of[k]]
+            self.x_own = [
+                Copy(piece(TO_X, k), into(0, k), into(0, k), sems, 6 + k, device(TO_X))
+                for k in range(2)
             ]
-
-        def start(self):
-            for k in (1, 2, 3, 0):
-                self.pair[k].start()
+            self.y_own = [
+                Copy(piece(TO_Y, k), into(1, k), into(1, k), sems, 8 + k, device(TO_Y))
+                for k in range(2)
+            ]
+
+        def add_pair(self, k):
+            self.pair[k].arrive()
+            slot = member(self.steps_of[k])
+            total = self.part[slot].astype(F32) + self.pair_in[k].astype(F32)
+            self.part[slot] = total.astype(BF)
+
+        def add_far(self, step, k):
+            slot = member(step)
+            total = self.part[slot, self.rows_of[k], :].astype(F32) + self.far_in[k].astype(F32)
+            self.part[slot, self.rows_of[k], :] = total.astype(BF)
+
+        def give_far(self):
+            self.pair[3].start()
+            self.pair[1].start()
+
+        def send_far(self):
+            self.add_pair(3)
+            self.x_far.start()
+            self.y_far.start()
+            self.add_pair(1)
+            self.x_own[0].start()
+
+        def give_near(self):
+            self.pair[2].start()
+            self.pair[0].start()
+
+        def send_near(self):
+            self.add_pair(2)
+            self.y_own[1].start()
+
+        def steps(self):
+            return {0: self.give_far, 1: self.send_far, 2: self.give_near, 3: self.send_near}
 
         def middle(self):
-            for k, (dx, dy) in enumerate(CHIPS):
-                self.pair[k + 1].arrive()
-                total = self.part[member((dx, 0, dy))].astype(F32) + self.pair_in[k + 1].astype(F32)
-                self.onward[k] = total.astype(BF)
-                self.across[k].start()
+            self.x_far.arrive()
+            self.add_far(TO_Y, 0)
+            self.y_own[0].start()
+            self.y_far.arrive()
+            self.add_far(TO_X, 1)
+            self.x_own[1].start()
 
         def finish(self):
             self.pair[0].arrive()
             total = self.part[me].astype(F32) + self.pair_in[0].astype(F32)
-            for k in range(len(CHIPS)):
-                self.across[k].arrive()
-                total = total + self.chip_in[k].astype(F32)
-            return total
+            for copies in (self.x_own, self.y_own):
+                for copy in copies:
+                    copy.arrive()
+            return total + self.chip_in[0].astype(F32) + self.chip_in[1].astype(F32)
 
     class Spread:
         def __init__(self, source, target, sems):
@@ -587,31 +668,100 @@
             for copy in self.copies:
                 copy.arrive()
 
+    class Relay:
+        def __init__(self, buffer, sems):
+            self.copies = {
+                along: Copy(
+                    buffer.at[z],
+                    buffer.at[z],
+                    buffer.at[jnp.clip(z - along, 0, lines - 1)],
+                    sems,
+                    at,
+                    line_device(along),
+                )
+                for at, along in enumerate((1, -1, 2, -2))
+            }
+            self.onward = {
+                along: Copy(
+                    buffer.at[far], buffer.at[far], buffer.at[far], sems, 4, line_device(along)
+                )
+                for along, far in ((1, 0), (-1, lines - 1))
+            }
+
+        def start(self):
+            for along in (2, -2, 1, -1):
+                self.copies[along].start(inside(along))
+
+        def middle(self):
+            @pl.when(z == 2)
+            def up_line():
+                self.copies[2].arrive()
+
+            @pl.when(z == 1)
+            def down_line():
+                self.copies[-2].arrive()
+
+            self.onward[1].start(z == 2)
+            self.onward[-1].start(z == 1)
+
+        def finish(self):
+            pl.when(z >= 1)(self.copies[1].arrive)
+            pl.when(z <= 2)(self.copies[-1].arrive)
+            pl.when(z == 3)(self.copies[2].arrive)
+            pl.when(z == 0)(self.copies[-2].arrive)
+            pl.when(z == 3)(self.onward[1].arrive)
+            pl.when(z == 0)(self.onward[-1].arrive)
+
     class Fold:
         def __init__(self, terms, landed, sems):
             self.terms, self.landed = terms, landed
-            self.copies = [
-                Copy(
-                    terms.at[(z + along) % lines],
-                    landed.at[along - 1],
-                    landed.at[along - 1],
+            self.copies = {
+                along: Copy(
+                    terms.at[jnp.clip(z + along, 0, lines - 1)],
+                    landed.at[min(at, 2)],
+                    landed.at[min(at, 2)],
                     sems,
-                    along - 1,
-                    device(here, along),
+                    at,
+                    line_device(along),
                 )
-                for along in range(1, lines)
-            ]
+                for at, along in enumerate((1, -1, 2, -2))
+            }
+            self.first = {
+                along: Copy(
+                    terms.at[far], landed.at[3], landed.at[3], sems, 4, line_device(along)
+                )
+                for along, far in ((1, lines - 1), (-1, 0))
+            }
 
         def start(self):
-            for copy in self.copies:
-                copy.start()
-
-        def finish(self):
-            total = self.terms[z].astype(F32)
-            for k, copy in enumerate(self.copies):
-                copy.arrive()
-                total = total + self.landed[k].astype(F32)
-            return total
+            self.first[1].start(z == 0)
+            self.first[-1].start(z == lines - 1)
+            self.copies[2].start(z == 0)
+            self.copies[-2].start(z == lines - 1)
+            for along in (1, -1):
+                self.copies[along].start(inside(along))
+
+        def middle(self):
+            for at, far, along in ((1, lines - 1, 1), (2, 0, -1)):
+
+                @pl.when(z == at)
+                def join():
+                    self.first[along].arrive()
+                    total = self.terms[far].astype(F32) + self.landed[3].astype(F32)
+                    self.terms[far] = total.astype(BF)
+
+                self.copies[2 * along].start(z == at)
+
+        def finish(self, total):
+            total[...] = self.terms[z].astype(F32)
+            for at, (along, when) in enumerate(((1, z >= 1), (-1, z <= 2), (2, z >= 2), (-2, z <= 1))):
+
+                @pl.when(when)
+                def add():
+                    self.copies[along].arrive()
+                    total[...] += self.landed[min(at, 2)].astype(F32)
+
+            return total[...]
 
     class Canvases:
         def __init__(self, buffer, sems):
@@ -655,12 +805,17 @@
             for copy in self.far:
                 copy.arrive()
 
-    def each_canvas(body, which=None):
-        if which is None:
-            lax.fori_loop(0, 4, lambda t, carry: (body(t), carry)[1], 0)
-        else:
-            base = c if which == 0 else 1 - c
-            lax.fori_loop(0, 2, lambda t, carry: (body(2 * t + base), carry)[1], 0)
+    def each_canvas(body, near=True, before=None, after=None):
+        def step(t, carry):
+            for k, action in (before or {}).items():
+                pl.when(t == k)(action)
+            turn = t if near else 3 - t
+            body(2 * ((x + (turn // 2)) % 2) + (c + turn) % 2)
+            for k, action in (after or {}).items():
+                pl.when(t == k)(action)
+            return carry
+
+        lax.fori_loop(0, 4, step, 0)
 
     def slots(t):
         return pl.ds(2 * t, 2)
@@ -685,6 +840,10 @@
             first_part, pltpu.roll(value, lanes - 8, 1), pltpu.roll(value, 8, 1)
         )
 
+    barrier = pltpu.get_barrier_semaphore()
+    partners = [device(step) for step in PLANE] + [device(here, k) for k in range(1, lines)]
+    for target in partners:
+        pl.semaphore_signal(barrier, inc=1, device_id=target, device_id_type=MESH)
     ids = s.ids
     ids[me] = jnp.zeros(ids.shape[1:], jnp.int32)
     ids[me, 0:1, :] = crop_ref[...]
@@ -702,32 +861,41 @@
     mod_full[0:mod_rows, 0:width] = amod_ref[...]
     mod_full[0:mod_rows, width : 2 * width] = fmod_ref[...]
 
-    barrier = pltpu.get_barrier_semaphore()
-    partners = [device(step) for step in PLANE] + [device(here, k) for k in range(1, lines)]
-    for target in partners:
-        pl.semaphore_signal(barrier, inc=1, device_id=target, device_id_type=MESH)
+    size = lanes // 2
+    qkv_places = [
+        (m, (2 * part + k) * size, part * width + (8 * (m % 2) + 4 * k + m // 2) * size)
+        for m in range(8)
+        for part in range(3)
+        for k in range(2)
+    ]
+    up_places = [
+        (m, (lines * part + k) * down_rows, part * 8 * hidden + (8 * k + m) * down_rows)
+        for m in range(8)
+        for part in range(2)
+        for k in range(lines)
+    ]
+    for m, own, whole in qkv_places:
+        s.qkv_cols[m, :, own : own + size] = qkv_ref[:, whole : whole + size]
+    for m, own, whole in up_places:
+        s.up_cols[m, :, own : own + down_rows] = up_ref[:, whole : whole + down_rows]
     pl.semaphore_wait(barrier, len(partners))
 
     cond_copy = Canvases(conds, s.sem_cond)
     ids_copy = Share(ids, s.sem_ids)
-    qkv_spread = Spread(qkv_ref, s.qkv_line.at[z], s.sem_qkv_spread)
-    up_spread = Spread(up_ref, s.up_line.at[z], s.sem_up_spread)
-    qkv_line = Line(s.qkv_line, s.sem_qkv_line)
-    out_line = Line(s.out_line, s.sem_out_line)
-    up_line = Line(s.up_line, s.sem_up_line)
-    down_line = Line(s.down_line, s.sem_down_line)
+    qkv_spread = Spread(s.qkv_cols, s.qkv_line.at[z], s.sem_qkv_spread)
+    up_spread = Spread(s.up_cols, s.up_line.at[z], s.sem_up_spread)
+    qkv_line = Relay(s.qkv_line, s.sem_qkv_line)
+    out_line = Relay(s.out_line, s.sem_out_line)
+    up_line = Relay(s.up_line, s.sem_up_line)
+    down_line = Relay(s.down_line, s.sem_down_line)
     token_copy = Gather(s.tokens, s.sem_tokens)
     cot_copy = Gather(s.cots, s.sem_cots)
     cond_copy.start()
     qkv_spread.start()
-    ids_copy.start()
+    cond_copy.middle()
     out_line.start()
-    token_copy.start()
-    cond_copy.middle()
     qkv_spread.finish()
     qkv_line.start()
-    up_spread.start()
-
     cond_copy.finish()
     picked = jnp.zeros((conds.shape[0], 128), F32)
     for r in range(cond_ref.shape[1] // 128):
@@ -744,7 +912,7 @@
         mod_terms[m] = dot(cond_mine, mod_full[:, block_cols * m : block_cols * (m + 1)])
     mod_spread = Spread(mod_terms, mod_in, s.sem_mod_spread)
     mod_spread.start()
-    token_copy.middle()
+    token_copy.start()
     mod_spread.finish()
     mod_sum = mod_in[0]
     for m in range(1, 8):
@@ -753,9 +921,8 @@
     mod_line[z] = mod_sum
     mod_copy = Line(mod_line, s.sem_mod_line)
     mod_copy.start()
-    up_spread.finish()
-    up_line.start()
-    down_line.start()
+    token_copy.turn()
+    out_line.middle()
     mod_copy.finish()
     mod_sum = mod_line[0]
     for k in range(1, lines):
@@ -765,13 +932,13 @@
     own_rows = s.mod_total[pl.ds(8 * (z // 2), 8), :]
     s.mods[me] = own_rows
     mod_share.start()
-    token_copy.finish()
+    up_spread.start()
+    ids_copy.start()
+    cot_copy.start()
     mod_share.finish()
     scales = s.scales
     for m in range(8):
         scales[:, block_cols * m : block_cols * (m + 1)] = s.mods[m]
-    cot_copy.start()
-    ids_copy.finish()
 
     def scale_row(canvas, ffn):
         row = scales[pl.ds(4 * (z % 2) + canvas, 1), :]
@@ -789,7 +956,11 @@
         scaled = value * inverse_rms(value) * scale_row(canvas, False)
         normed[slots(canvas)] = scaled.astype(BF).reshape(2, rows, width)
 
-    each_canvas(norm_tokens)
+    each_canvas(norm_tokens, before=token_copy.steps())
+    qkv_line.middle()
+    up_spread.finish()
+    up_line.start()
+    down_line.start()
     out_line.finish()
     out_half = s.out_half
     half_copy = Copy(
@@ -801,6 +972,8 @@
         device((0, 0, 1)),
     )
     half_copy.start()
+    cot_copy.turn()
+    ids_copy.finish()
     qkv_line.finish()
     head_of = lambda k: 8 * y + 4 * k + 2 * x + c
     head_scales = [scale_ref[head_of(k)] for k in range(2)]
@@ -864,20 +1037,19 @@
         s.mid_part[slots(canvas)] = value.astype(BF).reshape(2, rows, width)
 
     mid_reduce = Reduce(
-        s.mid_part, s.mid_pair, s.mid_onward, s.mid_chip, s.sem_mid
-    )
-    each_canvas(to_middle, 1)
-    mid_reduce.start()
-    each_canvas(to_middle, 0)
+        s.mid_part, s.mid_pair, s.mid_far, s.mid_chip, s.sem_mid
+    )
+    each_canvas(to_middle, False, after=mid_reduce.steps())
     mid_reduce.middle()
-    cot_copy.middle()
+    cot_copy.finish()
+    up_line.middle()
     middle = x_ref[...].astype(F32) + mid_reduce.finish()
     s.middle[...] = middle
     ffn_row = scale_row(own_canvas, True)
     s.ffn[me] = (middle * inverse_rms(middle) * ffn_row).astype(BF)
     ffn_copy = Gather(s.ffn, s.sem_ffn)
     ffn_copy.start()
-    cot_copy.finish()
+    ffn_copy.turn()
     up_line.finish()
 
     def feed(canvas):
@@ -893,10 +1065,8 @@
         density = jnp.exp(-0.5 * gate * gate) * (1.0 / math.sqrt(2.0 * math.pi))
         s.slope[canvas] = value * (cdf + gate * density)
 
-    ffn_copy.middle()
-    each_canvas(feed, 0)
-    ffn_copy.finish()
-    each_canvas(feed, 1)
+    each_canvas(feed, before=ffn_copy.steps())
+    down_line.middle()
 
     def cots_of(canvas):
         return s.cots[slots(canvas)].reshape(canvas_rows, width)
@@ -930,11 +1100,9 @@
         s.gnf_part[slots(canvas)] = part.astype(BF).reshape(2, rows, width)
 
     gnf_reduce = Reduce(
-        s.gnf_part, s.gnf_pair, s.gnf_onward, s.gnf_chip, s.sem_gnf
-    )
-    each_canvas(feed_back, 1)
-    gnf_reduce.start()
-    each_canvas(feed_back, 0)
+        s.gnf_part, s.gnf_pair, s.gnf_far, s.gnf_chip, s.sem_gnf
+    )
+    each_canvas(feed_back, False, after=gnf_reduce.steps())
     gnf_reduce.middle()
 
     def up_term(k, carry):
@@ -951,6 +1119,7 @@
     lax.fori_loop(0, lines, up_term, 0)
     up_fold = Fold(s.up_term, s.up_in, s.sem_up_fold)
     up_fold.start()
+    down_fold.middle()
 
     def norm_back(value, row, grad):
         inverse = inverse_rms(value)
@@ -977,11 +1146,14 @@
         s.out_part[slots(canvas)] = part.astype(BF).reshape(2, rows, width)
 
     out_reduce = Reduce(
-        s.out_part, s.out_pair, s.out_onward, s.out_chip, s.sem_out
-    )
+        s.out_part, s.out_pair, s.out_far, s.out_chip, s.sem_out
+    )
+    branch_copy.turn()
     each_canvas(to_out)
-    branch_copy.middle()
-    out_reduce.start()
+    up_fold.middle()
+    branch_copy.finish()
+    out_reduce.give_far()
+    out_reduce.give_near()
 
     def attend_back(canvas):
         branch = s.branch[slots(canvas)].reshape(canvas_rows, width)
@@ -1020,13 +1192,12 @@
         s.gna_part[slots(canvas)] = part.astype(BF).reshape(2, rows, width)
 
     s.head_terms[...] = jnp.zeros((1, lanes), F32)
-    branch_copy.finish()
     gna_reduce = Reduce(
-        s.gna_part, s.gna_pair, s.gna_onward, s.gna_chip, s.sem_gna
-    )
-    each_canvas(attend_back, 1)
-    gna_reduce.start()
-    each_canvas(attend_back, 0)
+        s.gna_part, s.gna_pair, s.gna_far, s.gna_chip, s.sem_gna
+    )
+    each_canvas(attend_back, False, after=gna_reduce.steps())
+    out_reduce.send_far()
+    out_reduce.send_near()
     gna_reduce.middle()
 
     def qkv_term(k, carry):
@@ -1085,18 +1256,20 @@
         out_terms[2 * (1 - y) + k] = s.out_swap[k]
     out_fold = Fold(out_terms, s.out_in, s.sem_out_fold)
     out_fold.start()
+    qkv_fold.middle()
     sums_copy.arrive()
     sums = s.sums
     sums[dp] = sums_own[...] + s.sums_pair[...]
     all_sums = Canvases(sums, s.sem_sums)
     all_sums.start()
-    down_grad[...] = down_fold.finish().reshape(down_rows, width)
+    down_grad[...] = down_fold.finish(s.down_total).reshape(down_rows, width)
     all_sums.middle()
+    out_fold.middle()
     block_out[...] = (s.middle[...] + out_reduce.finish()).astype(BF)
-    s.up_sum[...] = up_fold.finish().astype(BF)
+    s.up_sum[...] = up_fold.finish(s.up_total).astype(BF)
     up_return = Spread(s.up_sum, s.up_back, s.sem_up_back)
     up_return.start()
-    s.qkv_sum[...] = qkv_fold.finish().astype(BF)
+    s.qkv_sum[...] = qkv_fold.finish(s.qkv_total).astype(BF)
     qkv_return = Spread(s.qkv_sum, s.qkv_back, s.sem_qkv_back)
     qkv_return.start()
 
@@ -1131,29 +1304,35 @@
     head_sum = sums[0, 16:17, :]
     for k in range(1, sums.shape[0]):
         head_sum = head_sum + sums[k, 16:17, :]
-    scale_grad[...] = head_sum
+    scale_grad[...] = head_sum[:, : scale_grad.shape[1]]
     for copy in cond_send:
         copy.arrive()
     cond_share = Share(cond_in, s.sem_cond_share)
     cond_share.start()
-    out_grad[...] = out_fold.finish()
+    out_grad[...] = out_fold.finish(s.out_total)
     cond_share.finish()
     for k in range(lines):
         for m in range(8):
             at_row = 8 * k + m
-            cond_grad[at_row : at_row + 1, :] = cond_in[m, k, pl.ds(4 * (z % 2) + own_canvas, 1), :]
+            row = cond_in[m, k, pl.ds(4 * (z % 2) + own_canvas, 1), :]
+            cond_grad[:, at_row * mod_rows : (at_row + 1) * mod_rows] = row[:, :mod_rows]
     up_return.finish()
-    up_grad[...] = s.up_back[...]
+    for m, own, whole in up_places:
+        up_grad[:, whole : whole + down_rows] = s.up_back[m, :, own : own + down_rows].astype(F32)
     qkv_return.finish()
-    qkv_grad[...] = s.qkv_back[...]
-    for copy in sends:
-        copy.wait_send()
+    for m, own, whole in qkv_places:
+        qkv_grad[:, whole : whole + size] = s.qkv_back[m, :, own : own + size].astype(F32)
+    for copy, when in sends:
+        if when is None:
+            copy.wait_send()
+        else:
+            pl.when(when)(copy.wait_send)
 
 
 def scratch_plan(lines, x_ref, qkv_ref, up_ref, out_ref, down_ref):
     rows, width = x_ref.shape
-    own_cols = qkv_ref.shape[2]
-    up_rows, up_cols = up_ref.shape[1:]
+    up_rows = up_ref.shape[0]
+    own_cols, up_cols = qkv_ref.shape[1] // 8, up_ref.shape[1] // 8
     hidden = up_cols // 2
     half_head = out_ref.shape[0]
     down_rows = down_ref.shape[0]
@@ -1170,6 +1349,8 @@
         normed=vm(plane),
         ffn=vm(plane),
         branch=vm(plane),
+        qkv_cols=vm((8, up_rows, own_cols)),
+        up_cols=vm((8, up_rows, up_cols)),
         qkv_line=vm((lines, 8, up_rows, own_cols)),
         up_line=vm((lines, 8, up_rows, up_cols)),
         out_line=vm((lines, half_head, width)),
@@ -1203,32 +1384,36 @@
         cond_all=vm((groups, 128), F32),
         cond_line=vm((lines, 8, 128), F32),
         cond_in=vm((8, lines, 8, 128), F32),
+        down_total=vm((down_rows, width), F32),
+        up_total=vm((8, up_rows, up_cols), F32),
+        qkv_total=vm((8, up_rows, own_cols), F32),
+        out_total=vm((half_head, width), F32),
         down_term=vm((lines, down_rows, width)),
-        down_in=vm((lines - 1, down_rows, width)),
+        down_in=vm((4, down_rows, width)),
         up_term=vm((lines, 8, up_rows, up_cols)),
-        up_in=vm((lines - 1, 8, up_rows, up_cols)),
+        up_in=vm((4, 8, up_rows, up_cols)),
         up_sum=vm((8, up_rows, up_cols)),
         up_back=vm((8, up_rows, up_cols)),
         qkv_term=vm((lines, 8, up_rows, own_cols)),
-        qkv_in=vm((lines - 1, 8, up_rows, own_cols)),
+        qkv_in=vm((4, 8, up_rows, own_cols)),
         qkv_sum=vm((8, up_rows, own_cols)),
         qkv_back=vm((8, up_rows, own_cols)),
         out_halves=vm((2, 2, half_head, width)),
         out_swap=vm((2, half_head, width)),
         out_terms=vm((lines, half_head, width)),
-        out_in=vm((lines - 1, half_head, width)),
+        out_in=vm((4, half_head, width)),
     )
     for name in ("mid", "gnf", "out", "gna"):
         plan[name + "_part"] = vm(plane)
         plan[name + "_pair"] = vm((4, rows, width))
-        plan[name + "_onward"] = vm((3, rows, width))
-        plan[name + "_chip"] = vm((3, rows, width))
-        plan["sem_" + name] = sem(7)
+        plan[name + "_far"] = vm((2, rows // 2, width))
+        plan[name + "_chip"] = vm((2, rows, width))
+        plan["sem_" + name] = sem(10)
     plan.update(
-        sem_tokens=sem(7),
-        sem_cots=sem(7),
-        sem_ffn=sem(7),
-        sem_branch=sem(7),
+        sem_tokens=sem(10),
+        sem_cots=sem(10),
+        sem_ffn=sem(10),
+        sem_branch=sem(10),
         sem_ids=sem(7),
         sem_qkv_spread=sem(7),
         sem_up_spread=sem(7),
@@ -1237,16 +1422,16 @@
         sem_up_back=sem(7),
         sem_qkv_back=sem(7),
         sem_cond_share=sem(7),
-        sem_qkv_line=sem(lines - 1),
-        sem_up_line=sem(lines - 1),
-        sem_out_line=sem(lines - 1),
-        sem_down_line=sem(lines - 1),
+        sem_qkv_line=sem(5),
+        sem_up_line=sem(5),
+        sem_out_line=sem(5),
+        sem_down_line=sem(5),
         sem_mod_line=sem(lines - 1),
         sem_cond_line=sem(lines - 1),
-        sem_down_fold=sem(lines - 1),
-        sem_up_fold=sem(lines - 1),
-        sem_qkv_fold=sem(lines - 1),
-        sem_out_fold=sem(lines - 1),
+        sem_down_fold=sem(5),
+        sem_up_fold=sem(5),
+        sem_qkv_fold=sem(5),
+        sem_out_fold=sem(5),
         sem_cond=sem(lines + 2),
         sem_sums=sem(lines + 2),
         sem_half=sem(3),
@@ -1295,19 +1480,13 @@
     lines = lax.axis_size("dp") // 4
     rows, width = block_in.shape[1:]
     heads = head_scale.shape[0]
-    up_rows = qkv_weight.shape[0]
-    own_hidden = down_weight.shape[0]
-    qkv = qkv_weight.reshape(up_rows, 3, 2, 2, 2, 2, 64).transpose(4, 5, 2, 0, 1, 3, 6)
-    qkv = qkv.reshape(8, up_rows, -1)
-    up = up_weight.reshape(up_rows, 2, lines, 8, own_hidden).transpose(3, 0, 1, 2, 4)
-    up = up.reshape(8, up_rows, -1)
     tables = jnp.asarray(turn_tables(heads, lines))
     kinds = jax.ShapeDtypeStruct
     operands = (
         block_in[0],
         cotangent[0],
-        qkv,
-        up,
+        qkv_weight,
+        up_weight,
         out_weight,
         down_weight,
         attn_modulate,
@@ -1318,7 +1497,7 @@
         head_scale,
         tables,
     )
-    plan = scratch_plan(lines, operands[0], qkv, up, out_weight, down_weight)
+    plan = scratch_plan(lines, operands[0], qkv_weight, up_weight, out_weight, down_weight)
     in_vmem = pl.BlockSpec(memory_space=pltpu.VMEM)
     in_specs = [in_vmem] * len(operands)
     in_specs[11] = pl.BlockSpec(memory_space=pltpu.SMEM)
@@ -1327,14 +1506,14 @@
         out_shape=(
             kinds((rows, width), BF),
             kinds((rows, width), F32),
-            kinds((8 * lines, 128), F32),
-            kinds(qkv.shape, BF),
+            kinds(conditioning.shape, F32),
+            kinds(qkv_weight.shape, F32),
             kinds(out_weight.shape, F32),
-            kinds(up.shape, BF),
+            kinds(up_weight.shape, F32),
             kinds(down_weight.shape, F32),
             kinds(attn_modulate.shape, F32),
             kinds(ffn_modulate.shape, F32),
-            kinds((1, 128), F32),
+            kinds((1, heads), F32),
         ),
         in_specs=in_specs,
         out_specs=[in_vmem] * 10,
@@ -1343,25 +1522,30 @@
             collective_id=0, has_side_effects=True, vmem_limit_bytes=63 * 2**20
         ),
     )(*operands)
-    block_out, input_grad, cond, qkv_back, out_grad, up_back, down_grad, amod, fmod, scale = results
-    mod_rows = attn_modulate.shape[0]
-    cond_grad = cond[:, :mod_rows].reshape(1, -1)
-    qkv_grad = qkv_back.reshape(2, 2, 2, up_rows, 3, 2, 64).transpose(3, 4, 2, 5, 0, 1, 6)
-    qkv_grad = qkv_grad.reshape(qkv_weight.shape).astype(F32)
-    up_grad = up_back.reshape(8, up_rows, 2, lines, own_hidden).transpose(1, 2, 3, 0, 4)
-    up_grad = up_grad.reshape(up_weight.shape).astype(F32)
-    return (
-        block_out[None],
-        input_grad[None],
-        cond_grad,
-        qkv_grad,
-        out_grad,
-        up_grad,
-        down_grad,
-        amod,
-        fmod,
-        scale[0, :heads],
-    )
+    results = settle(results)
+    return tuple(item[None] for item in results[:2]) + tuple(results[2:-1]) + (results[-1][0],)
+
+
+def settle(results):
+    count = len(results)
+
+    def kernel(*refs):
+        copies = [
+            pltpu.make_async_copy(refs[k], refs[count + k], refs[-1].at[k]) for k in range(count)
+        ]
+        for copy in copies:
+            copy.start()
+        for copy in copies:
+            copy.wait()
+
+    anywhere = pl.BlockSpec(memory_space=pl.ANY)
+    return pl.pallas_call(
+        kernel,
+        out_shape=tuple(jax.ShapeDtypeStruct(item.shape, item.dtype) for item in results),
+        in_specs=[pl.BlockSpec(memory_space=pltpu.VMEM)] * count,
+        out_specs=[anywhere] * count,
+        scratch_shapes=[pltpu.SemaphoreType.DMA((count,))],
+    )(*results)
 
 
 def in_planes(mesh):

time: 214 us -> 164 us (0.77)
  Pallas kernels: 196 us -> 163 us
  local copies, waits for them, and re-layouts: 17 us -> 0 us
    pallas_call x1, Pallas kernels: 196 us -> 159 us  [plane_shards(): pl.pallas_call(functools.partial(block_kernel, lines), out_shape=(kinds((...]
    convert_element_type x6 -> x0, local copies, waits for them, and re-layouts: 6.51 us -> none  [the longest x3 3.95 us: plane_shards(): up_grad = up_grad.reshape(up_weight.shape).astype(F32)]
    reshape x7 -> x0, local copies, waits for them, and re-layouts: 5.08 us -> none  [the longest x2 1.72 us: plane_shards(): up_weight.reshape(up_rows, 2, lines, 8, own_hidden).transpose(3, 0, 1, 2, 4)]
    unnamed x26 -> x0, local copies, waits for them, and re-layouts: 4.92 us -> none
    pallas_call x0 -> x1, Pallas kernels: none -> 3.27 us  [settle(): pl.pallas_call(kernel, out_shape=tuple((jax.ShapeDtypeStruct(item.shape,...]
where the time goes in v2:
time: 164 us; the launch traced here: 163 us
  Pallas kernels  163 us (99%)
    pallas_call x1, Pallas kernels, plane_shards(): pl.pallas_call(functools.partial(block_kernel, lines), out_shape=(kinds((...  159 us

profile of v2, /device:TPU:0, one launch (start us, length us, event | category | flops | bytes accessed | tf_op | source)
XLA Modules:
  0.0 163.4 jit_solution(15492638176815574255)
XLA Ops:
  0.6 159.5 %shard_map.204 = (bf16[128,1024]{1,0:T(8,128)(2,1)}, f32[128,1024]{1,0:T(8,128)}, f32[1,768]{1,0:T(1,128)}, f32[32,3072]{1,0:T(8,128)}, f32[32,1024]{1,0:T(8,128...) custom-call(bf16[128,1024]{1,0:T(8,128)(2,1)} %bitcast.5, ...), custom_call_target="tpu_custom_call" | custom-call | tf_op jit(solution)/shard_map/pallas_call | solution.py:1504
  160.1 3.3 %shard_map.205 = (bf16[128,1024]{1,0:T(8,128)(2,1)}, f32[128,1024]{1,0:T(8,128)}, f32[1,768]{1,0:T(1,128)}, f32[32,3072]{1,0:T(8,128)}, f32[32,1024]{1,0:T(8,128...) custom-call(bf16[128,1024]{1,0:T(8,128)(2,1)} %get-tuple-element.30., ...), custom_call_target="tpu_custom_call" | custom-call | tf_op jit(solution)/shard_map/pallas_call | solution.py:1542

commit v3 on v2

--- a/solution.py
+++ b/solution.py
@@ -688,8 +688,8 @@
                 for along, far in ((1, 0), (-1, lines - 1))
             }
 
-        def start(self):
-            for along in (2, -2, 1, -1):
+        def start(self, steps=(2, -2, 1, -1)):
+            for along in steps:
                 self.copies[along].start(inside(along))
 
         def middle(self):
@@ -884,18 +884,21 @@
     ids_copy = Share(ids, s.sem_ids)
     qkv_spread = Spread(s.qkv_cols, s.qkv_line.at[z], s.sem_qkv_spread)
     up_spread = Spread(s.up_cols, s.up_line.at[z], s.sem_up_spread)
-    qkv_line = Relay(s.qkv_line, s.sem_qkv_line)
+    qkv_line = [
+        Relay(s.qkv_line.at[:, pl.ds(4 * k, 4)], s.sem_qkv_line.at[k]) for k in range(2)
+    ]
     out_line = Relay(s.out_line, s.sem_out_line)
-    up_line = Relay(s.up_line, s.sem_up_line)
+    up_line = [Relay(s.up_line.at[:, pl.ds(4 * k, 4)], s.sem_up_line.at[k]) for k in range(2)]
     down_line = Relay(s.down_line, s.sem_down_line)
     token_copy = Gather(s.tokens, s.sem_tokens)
     cot_copy = Gather(s.cots, s.sem_cots)
     cond_copy.start()
     qkv_spread.start()
+    token_copy.start()
     cond_copy.middle()
     out_line.start()
     qkv_spread.finish()
-    qkv_line.start()
+    qkv_line[0].start()
     cond_copy.finish()
     picked = jnp.zeros((conds.shape[0], 128), F32)
     for r in range(cond_ref.shape[1] // 128):
@@ -912,7 +915,7 @@
         mod_terms[m] = dot(cond_mine, mod_full[:, block_cols * m : block_cols * (m + 1)])
     mod_spread = Spread(mod_terms, mod_in, s.sem_mod_spread)
     mod_spread.start()
-    token_copy.start()
+    token_copy.turn()
     mod_spread.finish()
     mod_sum = mod_in[0]
     for m in range(1, 8):
@@ -921,8 +924,10 @@
     mod_line[z] = mod_sum
     mod_copy = Line(mod_line, s.sem_mod_line)
     mod_copy.start()
-    token_copy.turn()
-    out_line.middle()
+    qkv_line[1].start()
+    up_spread.start()
+    ids_copy.start()
+    qkv_line[0].middle()
     mod_copy.finish()
     mod_sum = mod_line[0]
     for k in range(1, lines):
@@ -932,9 +937,8 @@
     own_rows = s.mod_total[pl.ds(8 * (z // 2), 8), :]
     s.mods[me] = own_rows
     mod_share.start()
-    up_spread.start()
-    ids_copy.start()
     cot_copy.start()
+    out_line.middle()
     mod_share.finish()
     scales = s.scales
     for m in range(8):
@@ -957,10 +961,10 @@
         normed[slots(canvas)] = scaled.astype(BF).reshape(2, rows, width)
 
     each_canvas(norm_tokens, before=token_copy.steps())
-    qkv_line.middle()
+    qkv_line[1].middle()
     up_spread.finish()
-    up_line.start()
-    down_line.start()
+    for line in up_line:
+        line.start()
     out_line.finish()
     out_half = s.out_half
     half_copy = Copy(
@@ -974,7 +978,8 @@
     half_copy.start()
     cot_copy.turn()
     ids_copy.finish()
-    qkv_line.finish()
+    for line in qkv_line:
+        line.finish()
     head_of = lambda k: 8 * y + 4 * k + 2 * x + c
     head_scales = [scale_ref[head_of(k)] for k in range(2)]
     scale_lanes = per_head(head_scales)
@@ -1023,26 +1028,24 @@
             heads.append(dot(probs.astype(BF), values))
         attended = per_head(heads)
         s.raw_attended[canvas] = attended
-        s.attended[canvas] = attended.astype(BF)
-
-    each_canvas(attend)
+        attended = attended.astype(BF)
+        s.attended[canvas] = attended
+        value = dot(attended, out_full[...].reshape(lanes, width))
+        s.mid_part[slots(canvas)] = value.astype(BF).reshape(2, rows, width)
+
     half_copy.arrive()
     out_full = s.out_full
     for k in range(2):
         out_full[k, y] = s.out_line[2 * y + k]
         out_full[k, 1 - y] = out_half[k]
 
-    def to_middle(canvas):
-        value = dot(s.attended[canvas], out_full[...].reshape(lanes, width))
-        s.mid_part[slots(canvas)] = value.astype(BF).reshape(2, rows, width)
-
     mid_reduce = Reduce(
         s.mid_part, s.mid_pair, s.mid_far, s.mid_chip, s.sem_mid
     )
-    each_canvas(to_middle, False, after=mid_reduce.steps())
+    each_canvas(attend, False, after=mid_reduce.steps())
     mid_reduce.middle()
     cot_copy.finish()
-    up_line.middle()
+    up_line[0].middle()
     middle = x_ref[...].astype(F32) + mid_reduce.finish()
     s.middle[...] = middle
     ffn_row = scale_row(own_canvas, True)
@@ -1050,7 +1053,10 @@
     ffn_copy = Gather(s.ffn, s.sem_ffn)
     ffn_copy.start()
     ffn_copy.turn()
-    up_line.finish()
+    up_line[1].middle()
+    down_line.start()
+    for line in up_line:
+        line.finish()
 
     def feed(canvas):
         up = dot(
@@ -1150,7 +1156,6 @@
     )
     branch_copy.turn()
     each_canvas(to_out)
-    up_fold.middle()
     branch_copy.finish()
     out_reduce.give_far()
     out_reduce.give_near()
@@ -1191,30 +1196,6 @@
         part = dot(grad_qkv, s.qkv_line[...].reshape(width, own_cols), 1, 1)
         s.gna_part[slots(canvas)] = part.astype(BF).reshape(2, rows, width)
 
-    s.head_terms[...] = jnp.zeros((1, lanes), F32)
-    gna_reduce = Reduce(
-        s.gna_part, s.gna_pair, s.gna_far, s.gna_chip, s.sem_gna
-    )
-    each_canvas(attend_back, False, after=gna_reduce.steps())
-    out_reduce.send_far()
-    out_reduce.send_near()
-    gna_reduce.middle()
-
-    def qkv_term(k, carry):
-        cols = pl.ds(pl.multiple_of(k * 8 * up_rows, 8 * up_rows), 8 * up_rows)
-        term = dot(
-            normed[:, :, cols].reshape(all_rows, 8 * up_rows),
-            s.grad_qkv[...].reshape(all_rows, own_cols),
-            0,
-            0,
-        )
-        s.qkv_term[k] = term.astype(BF).reshape(8, up_rows, own_cols)
-        return carry
-
-    lax.fori_loop(0, lines, qkv_term, 0)
-    qkv_fold = Fold(s.qkv_term, s.qkv_in, s.sem_qkv_fold)
-    qkv_fold.start()
-
     term = dot(
         s.attended[...].reshape(all_rows, lanes),
         s.branch[...].reshape(all_rows, width),
@@ -1230,6 +1211,38 @@
     )
     swap.start()
 
+    s.head_terms[...] = jnp.zeros((1, lanes), F32)
+    gna_reduce = Reduce(
+        s.gna_part, s.gna_pair, s.gna_far, s.gna_chip, s.sem_gna
+    )
+    each_canvas(attend_back, False, after=gna_reduce.steps())
+    up_fold.middle()
+    out_reduce.send_far()
+    out_reduce.send_near()
+    gna_reduce.middle()
+
+    swap.arrive()
+    out_terms = s.out_terms
+    for k in range(2):
+        out_terms[2 * y + k] = halves[y, k]
+        out_terms[2 * (1 - y) + k] = s.out_swap[k]
+    out_fold = Fold(out_terms, s.out_in, s.sem_out_fold)
+    out_fold.start()
+    def qkv_term(k, carry):
+        cols = pl.ds(pl.multiple_of(k * 8 * up_rows, 8 * up_rows), 8 * up_rows)
+        term = dot(
+            normed[:, :, cols].reshape(all_rows, 8 * up_rows),
+            s.grad_qkv[...].reshape(all_rows, own_cols),
+            0,
+            0,
+        )
+        s.qkv_term[k] = term.astype(BF).reshape(8, up_rows, own_cols)
+        return carry
+
+    lax.fori_loop(0, lines, qkv_term, 0)
+    qkv_fold = Fold(s.qkv_term, s.qkv_in, s.sem_qkv_fold)
+    qkv_fold.start()
+
     grad_in, attn_sum = norm_back(x_ref[...].astype(F32), scale_row(own_canvas, False), gna_reduce.finish())
     input_grad[...] = s.grad_middle[...] + grad_in
     put_row(sums_own, 0, attn_sum)
@@ -1249,13 +1262,6 @@
     )
     sums_copy.start()
     out_reduce.middle()
-    swap.arrive()
-    out_terms = s.out_terms
-    for k in range(2):
-        out_terms[2 * y + k] = halves[y, k]
-        out_terms[2 * (1 - y) + k] = s.out_swap[k]
-    out_fold = Fold(out_terms, s.out_in, s.sem_out_fold)
-    out_fold.start()
     qkv_fold.middle()
     sums_copy.arrive()
     sums = s.sums
@@ -1269,6 +1275,9 @@
     s.up_sum[...] = up_fold.finish(s.up_total).astype(BF)
     up_return = Spread(s.up_sum, s.up_back, s.sem_up_back)
     up_return.start()
+    up_return.finish()
+    for m, own, whole in up_places:
+        up_grad[:, whole : whole + down_rows] = s.up_back[m, :, own : own + down_rows].astype(F32)
     s.qkv_sum[...] = qkv_fold.finish(s.qkv_total).astype(BF)
     qkv_return = Spread(s.qkv_sum, s.qkv_back, s.sem_qkv_back)
     qkv_return.start()
@@ -1310,18 +1319,15 @@
     cond_share = Share(cond_in, s.sem_cond_share)
     cond_share.start()
     out_grad[...] = out_fold.finish(s.out_total)
+    qkv_return.finish()
+    for m, own, whole in qkv_places:
+        qkv_grad[:, whole : whole + size] = s.qkv_back[m, :, own : own + size].astype(F32)
     cond_share.finish()
     for k in range(lines):
         for m in range(8):
             at_row = 8 * k + m
             row = cond_in[m, k, pl.ds(4 * (z % 2) + own_canvas, 1), :]
             cond_grad[:, at_row * mod_rows : (at_row + 1) * mod_rows] = row[:, :mod_rows]
-    up_return.finish()
-    for m, own, whole in up_places:
-        up_grad[:, whole : whole + down_rows] = s.up_back[m, :, own : own + down_rows].astype(F32)
-    qkv_return.finish()
-    for m, own, whole in qkv_places:
-        qkv_grad[:, whole : whole + size] = s.qkv_back[m, :, own : own + size].astype(F32)
     for copy, when in sends:
         if when is None:
             copy.wait_send()
@@ -1422,8 +1428,8 @@
         sem_up_back=sem(7),
         sem_qkv_back=sem(7),
         sem_cond_share=sem(7),
-        sem_qkv_line=sem(5),
-        sem_up_line=sem(5),
+        sem_qkv_line=pltpu.SemaphoreType.DMA((2, 2, 5)),
+        sem_up_line=pltpu.SemaphoreType.DMA((2, 2, 5)),
         sem_out_line=sem(5),
         sem_down_line=sem(5),
         sem_mod_line=sem(lines - 1),

time: 164 us -> 154 us (0.939)
  Pallas kernels: 163 us -> 153 us
    pallas_call x1, Pallas kernels: 159 us -> 150 us  [plane_shards(): pl.pallas_call(functools.partial(block_kernel, lines), out_shape=(kinds((...]
where the time goes in v3:
time: 154 us
  Pallas kernels  153 us (99%)
    pallas_call x1, Pallas kernels, plane_shards(): pl.pallas_call(functools.partial(block_kernel, lines), out_shape=(kinds((...  150 us
    pallas_call x1, Pallas kernels, settle(): pl.pallas_call(kernel, out_shape=tuple((jax.ShapeDtypeStruct(item.shape,...  3.27 us

profile of v3, /device:TPU:0, one launch (start us, length us, event | category | flops | bytes accessed | tf_op | source)
XLA Modules:
  0.0 153.8 jit_solution(13326752403734651345)
XLA Ops:
  0.6 149.7 %shard_map.204 = (bf16[128,1024]{1,0:T(8,128)(2,1)}, f32[128,1024]{1,0:T(8,128)}, f32[1,768]{1,0:T(1,128)}, f32[32,3072]{1,0:T(8,128)}, f32[32,1024]{1,0:T(8,128...) custom-call(bf16[128,1024]{1,0:T(8,128)(2,1)} %bitcast.5, ...), custom_call_target="tpu_custom_call" | custom-call | tf_op jit(solution)/shard_map/pallas_call | solution.py:1510
  150.3 3.3 %shard_map.205 = (bf16[128,1024]{1,0:T(8,128)(2,1)}, f32[128,1024]{1,0:T(8,128)}, f32[1,768]{1,0:T(1,128)}, f32[32,3072]{1,0:T(8,128)}, f32[32,1024]{1,0:T(8,128...) custom-call(bf16[128,1024]{1,0:T(8,128)(2,1)} %get-tuple-element.30., ...), custom_call_target="tpu_custom_call" | custom-call | tf_op jit(solution)/shard_map/pallas_call | solution.py:1548

commit v4 on v3

--- a/solution.py
+++ b/solution.py
@@ -329,6 +329,12 @@
 BF = jnp.bfloat16
 F32 = jnp.float32
 PLANE = ((1, 0, 0), (0, 0, 1), (1, 0, 1), (0, 1, 0), (1, 1, 0), (0, 1, 1), (1, 1, 1))
+SAME_Y = tuple(
+    (step, along)
+    for along in (1, 3, 2, 0)
+    for step in ((0, 0, 0), (1, 0, 0), (0, 1, 0), (1, 1, 0))
+    if along or step != (0, 0, 0)
+)
 TO_X, TO_Y, TO_FAR = (1, 0, 0), (0, 0, 1), (1, 0, 1)
 ERF_P = (
     0.00022905065861350646,
@@ -765,44 +771,26 @@
 
     class Canvases:
         def __init__(self, buffer, sems):
-            self.near = [
-                Copy(
-                    buffer.at[dp],
-                    buffer.at[dp],
-                    buffer.at[device(step)[0]],
-                    sems,
-                    k,
-                    device(step),
-                )
-                for k, step in enumerate(((1, 0, 0), (0, 1, 0), (1, 1, 0)))
-            ]
-            self.far = []
-            for along in range(1, lines):
-                back = (z + lines - along) % lines
-                mine = buffer.at[pl.ds(4 * z, 4)]
-                self.far.append(
+            self.copies = []
+            for at, (step, along) in enumerate(SAME_Y):
+                from_there = device(step, lines - along)[0]
+                self.copies.append(
                     Copy(
-                        mine,
-                        mine,
-                        buffer.at[pl.ds(4 * back, 4)],
+                        buffer.at[dp],
+                        buffer.at[dp],
+                        buffer.at[from_there],
                         sems,
-                        2 + along,
-                        device(here, along),
+                        at,
+                        device(step, along),
                     )
                 )
 
         def start(self):
-            for copy in self.near:
+            for copy in self.copies:
                 copy.start()
 
-        def middle(self):
-            for copy in self.near:
-                copy.arrive()
-            for copy in self.far:
-                copy.start()
-
         def finish(self):
-            for copy in self.far:
+            for copy in self.copies:
                 copy.arrive()
 
     def each_canvas(body, near=True, before=None, after=None):
@@ -841,7 +829,8 @@
         )
 
     barrier = pltpu.get_barrier_semaphore()
-    partners = [device(step) for step in PLANE] + [device(here, k) for k in range(1, lines)]
+    partners = [device(step) for step in PLANE if step[2]]
+    partners += [device(step, along) for step, along in SAME_Y]
     for target in partners:
         pl.semaphore_signal(barrier, inc=1, device_id=target, device_id_type=MESH)
     ids = s.ids
@@ -895,7 +884,6 @@
     cond_copy.start()
     qkv_spread.start()
     token_copy.start()
-    cond_copy.middle()
     out_line.start()
     qkv_spread.finish()
     qkv_line[0].start()
@@ -1240,8 +1228,12 @@
         return carry
 
     lax.fori_loop(0, lines, qkv_term, 0)
-    qkv_fold = Fold(s.qkv_term, s.qkv_in, s.sem_qkv_fold)
-    qkv_fold.start()
+    cuts = (pl.ds(0, 6), pl.ds(6, 2))
+    qkv_fold = [
+        Fold(s.qkv_term.at[:, cut], s.qkv_in.at[:, cut], s.sem_qkv_fold.at[k])
+        for k, cut in enumerate(cuts)
+    ]
+    qkv_fold[0].start()
 
     grad_in, attn_sum = norm_back(x_ref[...].astype(F32), scale_row(own_canvas, False), gna_reduce.finish())
     input_grad[...] = s.grad_middle[...] + grad_in
@@ -1257,20 +1249,20 @@
             (head_rows == 0) & (head_lane == head_of(k)), value, 0.0
         )
     sums_own[16:24, :] = head_tile
-    sums_copy = Copy(
-        sums_own, s.sums_pair, s.sums_pair, s.sem_half, 2, device((0, 0, 1))
-    )
-    sums_copy.start()
+    s.sums_plane[me] = sums_own[...]
+    sums_share = Share(s.sums_plane, s.sem_sums_share)
+    sums_share.start()
     out_reduce.middle()
-    qkv_fold.middle()
-    sums_copy.arrive()
+    out_fold.middle()
+    sums_share.finish()
     sums = s.sums
-    sums[dp] = sums_own[...] + s.sums_pair[...]
-    all_sums = Canvases(sums, s.sem_sums)
+    for k in range(4):
+        sums[4 * z + k] = s.sums_plane[2 * k] + s.sums_plane[2 * k + 1]
+    all_sums = Line(sums, s.sem_sums, 4)
     all_sums.start()
+    qkv_fold[1].start()
+    qkv_fold[0].middle()
     down_grad[...] = down_fold.finish(s.down_total).reshape(down_rows, width)
-    all_sums.middle()
-    out_fold.middle()
     block_out[...] = (s.middle[...] + out_reduce.finish()).astype(BF)
     s.up_sum[...] = up_fold.finish(s.up_total).astype(BF)
     up_return = Spread(s.up_sum, s.up_back, s.sem_up_back)
@@ -1278,7 +1270,9 @@
     up_return.finish()
     for m, own, whole in up_places:
         up_grad[:, whole : whole + down_rows] = s.up_back[m, :, own : own + down_rows].astype(F32)
-    s.qkv_sum[...] = qkv_fold.finish(s.qkv_total).astype(BF)
+    qkv_fold[1].middle()
+    for fold, cut in zip(qkv_fold, cuts):
+        s.qkv_sum[cut] = fold.finish(s.qkv_total.at[cut]).astype(BF)
     qkv_return = Spread(s.qkv_sum, s.qkv_back, s.sem_qkv_back)
     qkv_return.start()
 
@@ -1385,7 +1379,7 @@
         grad_qkv=vm((4, 2 * rows, own_cols)),
         head_terms=vm((1, lanes), F32),
         sums_own=vm((24, 128), F32),
-        sums_pair=vm((24, 128), F32),
+        sums_plane=vm((8, 24, 128), F32),
         sums=vm((groups, 24, 128), F32),
         cond_all=vm((groups, 128), F32),
         cond_line=vm((lines, 8, 128), F32),
@@ -1436,11 +1430,12 @@
         sem_cond_line=sem(lines - 1),
         sem_down_fold=sem(5),
         sem_up_fold=sem(5),
-        sem_qkv_fold=sem(5),
+        sem_qkv_fold=pltpu.SemaphoreType.DMA((2, 2, 5)),
         sem_out_fold=sem(5),
-        sem_cond=sem(lines + 2),
-        sem_sums=sem(lines + 2),
-        sem_half=sem(3),
+        sem_cond=sem(15),
+        sem_sums=sem(lines - 1),
+        sem_sums_share=sem(7),
+        sem_half=sem(2),
     )
     return plan
 
@@ -1536,21 +1531,29 @@
     count = len(results)
 
     def kernel(*refs):
-        copies = [
-            pltpu.make_async_copy(refs[k], refs[count + k], refs[-1].at[k]) for k in range(count)
+        held, sems = refs[2 * count : -1], refs[-1]
+        loads = [
+            pltpu.make_async_copy(refs[k], held[k], sems.at[0, k]) for k in range(count)
         ]
-        for copy in copies:
+        stores = [
+            pltpu.make_async_copy(held[k], refs[count + k], sems.at[1, k]) for k in range(count)
+        ]
+        for copy in loads:
             copy.start()
-        for copy in copies:
+        for load, store in zip(loads, stores):
+            load.wait()
+            store.start()
+        for copy in stores:
             copy.wait()
 
     anywhere = pl.BlockSpec(memory_space=pl.ANY)
     return pl.pallas_call(
         kernel,
         out_shape=tuple(jax.ShapeDtypeStruct(item.shape, item.dtype) for item in results),
-        in_specs=[pl.BlockSpec(memory_space=pltpu.VMEM)] * count,
+        in_specs=[anywhere] * count,
         out_specs=[anywhere] * count,
-        scratch_shapes=[pltpu.SemaphoreType.DMA((count,))],
+        scratch_shapes=[pltpu.VMEM(item.shape, item.dtype) for item in results]
+        + [pltpu.SemaphoreType.DMA((2, count))],
     )(*results)
 
 

time: 154 us -> 152 us (0.987)
  Pallas kernels: 153 us -> 151 us
where the time goes in v4:
time: 152 us
  Pallas kernels  151 us (99%)
    pallas_call x1, Pallas kernels, plane_shards(): pl.pallas_call(functools.partial(block_kernel, lines), out_shape=(kinds((...  149 us

profile of v4, /device:TPU:0, one launch (start us, length us, event | category | flops | bytes accessed | tf_op | source)
XLA Modules:
  0.0 152.2 jit_solution(6335147175552336706)
XLA Ops:
  0.6 148.6 %shard_map.204 = (bf16[128,1024]{1,0:T(8,128)(2,1)}, f32[128,1024]{1,0:T(8,128)}, f32[1,768]{1,0:T(1,128)}, f32[32,3072]{1,0:T(8,128)}, f32[32,1024]{1,0:T(8,128...) custom-call(bf16[128,1024]{1,0:T(8,128)(2,1)} %bitcast.5, ...), custom_call_target="tpu_custom_call" | custom-call | tf_op jit(solution)/shard_map/pallas_call | solution.py:1505
  149.2 2.8 %shard_map.205 = (bf16[128,1024]{1,0:T(8,128)(2,1)}, f32[128,1024]{1,0:T(8,128)}, f32[1,768]{1,0:T(1,128)}, f32[32,3072]{1,0:T(8,128)}, f32[32,1024]{1,0:T(8,128...) custom-call(bf16[128,1024]{1,0:T(8,128)(2,1)} %get-tuple-element.30., ...), custom_call_target="tpu_custom_call" | custom-call | tf_op jit(solution)/shard_map/pallas_call | solution.py:1550

commit v5 on v4

--- a/solution.py
+++ b/solution.py
@@ -387,18 +387,13 @@
     pos_ref,
     scale_ref,
     table_ref,
-    block_out,
-    input_grad,
-    cond_grad,
-    qkv_grad,
-    out_grad,
-    up_grad,
-    down_grad,
-    amod_grad,
-    fmod_grad,
-    scale_grad,
-    *scratch,
+    *results_and_scratch,
 ):
+    targets, held = results_and_scratch[:10], results_and_scratch[10:20]
+    scratch, give_sems = results_and_scratch[20:-1], results_and_scratch[-1]
+    block_out, input_grad, cond_grad, qkv_grad, out_grad = held[:5]
+    up_grad, down_grad, amod_grad, fmod_grad, scale_grad = held[5:]
+    gives = [pltpu.make_async_copy(held[k], targets[k], give_sems.at[k]) for k in range(10)]
     names = list(scratch_plan(lines, x_ref, qkv_ref, up_ref, out_ref, down_ref))
     s = types.SimpleNamespace(**dict(zip(names, scratch)))
     dp = lax.axis_index("dp")
@@ -1237,6 +1232,7 @@
 
     grad_in, attn_sum = norm_back(x_ref[...].astype(F32), scale_row(own_canvas, False), gna_reduce.finish())
     input_grad[...] = s.grad_middle[...] + grad_in
+    gives[1].start()
     put_row(sums_own, 0, attn_sum)
     head_rows = lax.broadcasted_iota(jnp.int32, (8, lanes), 0)
     head_lane = lax.broadcasted_iota(jnp.int32, (8, lanes), 1)
@@ -1263,13 +1259,16 @@
     qkv_fold[1].start()
     qkv_fold[0].middle()
     down_grad[...] = down_fold.finish(s.down_total).reshape(down_rows, width)
+    gives[6].start()
     block_out[...] = (s.middle[...] + out_reduce.finish()).astype(BF)
+    gives[0].start()
     s.up_sum[...] = up_fold.finish(s.up_total).astype(BF)
     up_return = Spread(s.up_sum, s.up_back, s.sem_up_back)
     up_return.start()
     up_return.finish()
     for m, own, whole in up_places:
         up_grad[:, whole : whole + down_rows] = s.up_back[m, :, own : own + down_rows].astype(F32)
+    gives[5].start()
     qkv_fold[1].middle()
     for fold, cut in zip(qkv_fold, cuts):
         s.qkv_sum[cut] = fold.finish(s.qkv_total.at[cut]).astype(BF)
@@ -1303,30 +1302,38 @@
         copy.start()
     cond_in[me, z] = cond_line[z]
     amod_grad[...] = dot(cond_mine, rounded[0], 0, 0)[:mod_rows]
+    gives[7].start()
     fmod_grad[...] = dot(cond_mine, rounded[1], 0, 0)[:mod_rows]
+    gives[8].start()
     head_sum = sums[0, 16:17, :]
     for k in range(1, sums.shape[0]):
         head_sum = head_sum + sums[k, 16:17, :]
     scale_grad[...] = head_sum[:, : scale_grad.shape[1]]
+    gives[9].start()
     for copy in cond_send:
         copy.arrive()
     cond_share = Share(cond_in, s.sem_cond_share)
     cond_share.start()
     out_grad[...] = out_fold.finish(s.out_total)
+    gives[4].start()
     qkv_return.finish()
     for m, own, whole in qkv_places:
         qkv_grad[:, whole : whole + size] = s.qkv_back[m, :, own : own + size].astype(F32)
+    gives[3].start()
     cond_share.finish()
     for k in range(lines):
         for m in range(8):
             at_row = 8 * k + m
             row = cond_in[m, k, pl.ds(4 * (z % 2) + own_canvas, 1), :]
             cond_grad[:, at_row * mod_rows : (at_row + 1) * mod_rows] = row[:, :mod_rows]
+    gives[2].start()
     for copy, when in sends:
         if when is None:
             copy.wait_send()
         else:
             pl.when(when)(copy.wait_send)
+    for copy in gives:
+        copy.wait()
 
 
 def scratch_plan(lines, x_ref, qkv_ref, up_ref, out_ref, down_ref):
@@ -1502,23 +1509,26 @@
     in_vmem = pl.BlockSpec(memory_space=pltpu.VMEM)
     in_specs = [in_vmem] * len(operands)
     in_specs[11] = pl.BlockSpec(memory_space=pltpu.SMEM)
+    shapes = (
+    kinds((rows, width), BF),
+    kinds((rows, width), F32),
+    kinds(conditioning.shape, F32),
+    kinds(qkv_weight.shape, F32),
+    kinds(out_weight.shape, F32),
+    kinds(up_weight.shape, F32),
+    kinds(down_weight.shape, F32),
+    kinds(attn_modulate.shape, F32),
+    kinds(ffn_modulate.shape, F32),
+    kinds((1, heads), F32),
+)
     results = pl.pallas_call(
         functools.partial(block_kernel, lines),
-        out_shape=(
-            kinds((rows, width), BF),
-            kinds((rows, width), F32),
-            kinds(conditioning.shape, F32),
-            kinds(qkv_weight.shape, F32),
-            kinds(out_weight.shape, F32),
-            kinds(up_weight.shape, F32),
-            kinds(down_weight.shape, F32),
-            kinds(attn_modulate.shape, F32),
-            kinds(ffn_modulate.shape, F32),
-            kinds((1, heads), F32),
-        ),
+        out_shape=shapes,
         in_specs=in_specs,
-        out_specs=[in_vmem] * 10,
-        scratch_shapes=list(plan.values()),
+        out_specs=[pl.BlockSpec(memory_space=pl.ANY)] * 10,
+        scratch_shapes=[pltpu.VMEM(kind.shape, kind.dtype) for kind in shapes]
+        + list(plan.values())
+        + [pltpu.SemaphoreType.DMA((10,))],
         compiler_params=pltpu.CompilerParams(
             collective_id=0, has_side_effects=True, vmem_limit_bytes=63 * 2**20
         ),

time: 152 us -> 151 us (level)
  no operation moved by 1% of the time
where the time goes in v5:
time: 151 us
  Pallas kernels  150 us (99%)
    pallas_call x1, Pallas kernels, plane_shards(): pl.pallas_call(functools.partial(block_kernel, lines), out_shape=shapes,...  147 us

profile of v5, /device:TPU:0, one launch (start us, length us, event | category | flops | bytes accessed | tf_op | source)
XLA Modules:
  0.0 151.1 jit_solution(6942556219296102162)
XLA Ops:
  0.6 147.5 %shard_map.204 = (bf16[128,1024]{1,0:T(8,128)(2,1)}, f32[128,1024]{1,0:T(8,128)}, f32[1,768]{1,0:T(1,128)}, f32[32,3072]{1,0:T(8,128)}, f32[32,1024]{1,0:T(8,128...) custom-call(bf16[128,1024]{1,0:T(8,128)(2,1)} %bitcast.5, ...), custom_call_target="tpu_custom_call" | custom-call | tf_op jit(solution)/shard_map/pallas_call | solution.py:1524
  148.1 2.8 %shard_map.205 = (bf16[128,1024]{1,0:T(8,128)(2,1)}, f32[128,1024]{1,0:T(8,128)}, f32[1,768]{1,0:T(1,128)}, f32[32,3072]{1,0:T(8,128)}, f32[32,1024]{1,0:T(8,128...) custom-call(bf16[128,1024]{1,0:T(8,128)(2,1)} %get-tuple-element.30., ...), custom_call_target="tpu_custom_call" | custom-call | tf_op jit(solution)/shard_map/pallas_call | solution.py:1560

commit v6 on v5

--- a/solution.py
+++ b/solution.py
@@ -335,6 +335,8 @@
     for step in ((0, 0, 0), (1, 0, 0), (0, 1, 0), (1, 1, 0))
     if along or step != (0, 0, 0)
 )
+OTHERS = tuple((step, along) for along in (1, 3, 2) for step in ((0, 0, 0),) + PLANE)
+OTHERS += tuple((step, 0) for step in PLANE)
 TO_X, TO_Y, TO_FAR = (1, 0, 0), (0, 0, 1), (1, 0, 1)
 ERF_P = (
     0.00022905065861350646,
@@ -824,8 +826,7 @@
         )
 
     barrier = pltpu.get_barrier_semaphore()
-    partners = [device(step) for step in PLANE if step[2]]
-    partners += [device(step, along) for step, along in SAME_Y]
+    partners = [device(step, along) for step, along in OTHERS]
     for target in partners:
         pl.semaphore_signal(barrier, inc=1, device_id=target, device_id_type=MESH)
     ids = s.ids
@@ -1291,12 +1292,12 @@
         Copy(
             cond_line.at[(z + along) % lines],
             cond_in.at[me, z],
-            cond_in.at[me, (z + lines - along) % lines],
+            cond_in.at[member(step), (z + lines - along) % lines],
             s.sem_cond_line,
-            along - 1,
-            device(here, along),
-        )
-        for along in range(1, lines)
+            at,
+            device(step, along),
+        )
+        for at, (step, along) in enumerate(OTHERS)
     ]
     for copy in cond_send:
         copy.start()
@@ -1310,17 +1311,14 @@
         head_sum = head_sum + sums[k, 16:17, :]
     scale_grad[...] = head_sum[:, : scale_grad.shape[1]]
     gives[9].start()
-    for copy in cond_send:
-        copy.arrive()
-    cond_share = Share(cond_in, s.sem_cond_share)
-    cond_share.start()
     out_grad[...] = out_fold.finish(s.out_total)
     gives[4].start()
     qkv_return.finish()
     for m, own, whole in qkv_places:
         qkv_grad[:, whole : whole + size] = s.qkv_back[m, :, own : own + size].astype(F32)
     gives[3].start()
-    cond_share.finish()
+    for copy in cond_send:
+        copy.arrive()
     for k in range(lines):
         for m in range(8):
             at_row = 8 * k + m
@@ -1428,13 +1426,12 @@
         sem_mods=sem(7),
         sem_up_back=sem(7),
         sem_qkv_back=sem(7),
-        sem_cond_share=sem(7),
         sem_qkv_line=pltpu.SemaphoreType.DMA((2, 2, 5)),
         sem_up_line=pltpu.SemaphoreType.DMA((2, 2, 5)),
         sem_out_line=sem(5),
         sem_down_line=sem(5),
         sem_mod_line=sem(lines - 1),
-        sem_cond_line=sem(lines - 1),
+        sem_cond_line=sem(31),
         sem_down_fold=sem(5),
         sem_up_fold=sem(5),
         sem_qkv_fold=pltpu.SemaphoreType.DMA((2, 2, 5)),

time: 151 us -> 150 us (level)
  no operation moved by 1% of the time
where the time goes in v6:
time: 150 us
  Pallas kernels  149 us (99%)
    pallas_call x1, Pallas kernels, plane_shards(): pl.pallas_call(functools.partial(block_kernel, lines), out_shape=shapes,...  146 us

profile of v6, /device:TPU:0, one launch (start us, length us, event | category | flops | bytes accessed | tf_op | source)
XLA Modules:
  0.0 150.1 jit_solution(1845639672687383657)
XLA Ops:
  0.6 146.5 %shard_map.204 = (bf16[128,1024]{1,0:T(8,128)(2,1)}, f32[128,1024]{1,0:T(8,128)}, f32[1,768]{1,0:T(1,128)}, f32[32,3072]{1,0:T(8,128)}, f32[32,1024]{1,0:T(8,128...) custom-call(bf16[128,1024]{1,0:T(8,128)(2,1)} %bitcast.5, ...), custom_call_target="tpu_custom_call" | custom-call | tf_op jit(solution)/shard_map/pallas_call | solution.py:1521
  147.1 2.8 %shard_map.205 = (bf16[128,1024]{1,0:T(8,128)(2,1)}, f32[128,1024]{1,0:T(8,128)}, f32[1,768]{1,0:T(1,128)}, f32[32,3072]{1,0:T(8,128)}, f32[32,1024]{1,0:T(8,128...) custom-call(bf16[128,1024]{1,0:T(8,128)(2,1)} %get-tuple-element.30., ...), custom_call_target="tpu_custom_call" | custom-call | tf_op jit(solution)/shard_map/pallas_call | solution.py:1557
